TPU v7x, 256 devices: a whole 4x4x8 slice. The times are simulated.
256 devices in a mesh: gx: 16 (over z, core), gy: 16 (over x, y).
Axes of the slice: x: 4, y: 4, z: 8, core: 2. Of those that a mesh axis runs over, the one named last changes fastest.
Arguments:
- instruments: bfloat16 [64, 2048, 4096], P(None, 'gx', 'gy'), may hold values from -40 to 40
- regressors: bfloat16 [64, 2048, 4096], P(None, 'gx', 'gy'), may hold values from -6 to 6
- outcome: float32 [2048, 4096], P('gx', 'gy'), may hold values from -6 to 6
- land_mask: int32 [2048, 4096], P('gx', 'gy'), may hold values from 0 to 1, as said below
- coefficients: float32 [64], replicated, may hold values from -4 to 4
- weighting: float32 [64, 64], replicated, may hold values from -1 to 2, as said below
Outputs:
- smoothed: bfloat16 [64, 2048, 4096], P(None, 'gx', 'gy')
- hac_cov: float32 [64, 64], replicated
- new_coefficients: float32 [64], replicated
Inputs may be any that keep to these rules, and one draw needn't show every extreme that they name: `land_mask`: 1 marks land, 0 water. `weighting`: symmetric positive definite.
All inputs are finite; a program needn't handle non-finite values.
Results may differ from a plain program's by a relative error of at most 0.0012.
The roundings to bfloat16 on the way count: a program that leaves them out, or rounds other values in their place, can miss the bound.
Values may be sent and summed in bfloat16 or wider, within the bound.
A program may use at most 128 MiB of HBM per device.

v0:
```python
import jax
import jax.numpy as jnp
from jax import lax
from jax.sharding import PartitionSpec as P

B = 64


step_rate = 0.05


def padded_2(block, sides, width):
    for axis, dim in sides:
        count = lax.axis_size(axis)
        forward = [(i, i + 1) for i in range(count - 1)]
        backward = [(target, source) for source, target in forward]
        low = lax.ppermute(
            lax.slice_in_dim(block, block.shape[dim] - width, None, axis=dim), axis, forward
        )
        high = lax.ppermute(lax.slice_in_dim(block, 0, width, axis=dim), axis, backward)
        block = jnp.concatenate([low, block, high], axis=dim)
    return block


def band_matrix(length, radius):
    row_ids = lax.broadcasted_iota(jnp.int32, (length + 2 * radius, length), 0)
    col_ids = lax.broadcasted_iota(jnp.int32, (length + 2 * radius, length), 1)
    offset = jnp.abs(row_ids - col_ids - radius)
    return jnp.maximum(radius + 1 - offset, 0).astype(jnp.bfloat16)


def local(instruments, regressors, outcome, land_mask, coefficients, weighting):
    channels, rows_here, columns_here = instruments.shape
    radius = B
    half_coefficients = coefficients.astype(jnp.bfloat16)
    fitted = jnp.einsum(
        "pxy,p->xy", regressors, half_coefficients, preferred_element_type=jnp.float32
    )
    weighted = land_mask.astype(jnp.float32) * (outcome - fitted)
    moments = (instruments * weighted[None]).astype(jnp.bfloat16)
    land_half = land_mask.astype(jnp.bfloat16)
    band_second = band_matrix(columns_here, radius)
    band_first = band_matrix(rows_here, radius)
    padded = padded_2(moments, (("gx", 1), ("gy", 2)), radius)
    across = (
        jnp.einsum("kij,jb->kib", padded, band_second, preferred_element_type=jnp.float32)
        * (1.0 / (radius + 1))
    ).astype(jnp.bfloat16)
    summed = jnp.einsum("kib,ia->kab", across, band_first, preferred_element_type=jnp.float32)
    smoothed = (summed * (1.0 / (radius + 1) ** 2)).astype(jnp.bfloat16)
    products = lax.dot_general(
        moments.reshape(channels, -1),
        smoothed.reshape(channels, -1),
        (((1,), (1,)), ((), ())),
        preferred_element_type=jnp.float32,
    )
    flat_inst = instruments.reshape(channels, -1)
    flat_reg = (regressors * land_half[None]).reshape(regressors.shape[0], -1)
    cross_terms = lax.dot_general(
        flat_inst, flat_reg, (((1,), (1,)), ((), ())), preferred_element_type=jnp.float32
    )
    moment_sums = jnp.sum(moments, axis=(1, 2), dtype=jnp.float32)
    land_cells = jnp.sum(land_mask.astype(jnp.float32))
    cross_part = cross_terms
    moment_part = moment_sums
    land_part = land_cells
    cov_sum, cross_terms, moment_sums, land_cells = lax.psum(
        (products, cross_part, moment_part, land_part), ("gx", "gy")
    )
    hac_cov = cov_sum * ((radius + 1) / land_cells)
    mean_moment = moment_sums / land_cells
    jacobian = -cross_terms / land_cells
    gradient = 2.0 * jnp.dot(
        jacobian.T,
        jnp.dot(weighting, mean_moment, precision=lax.Precision.HIGHEST),
        precision=lax.Precision.HIGHEST,
    )
    new_coefficients = coefficients - step_rate * gradient
    return (smoothed, hac_cov, new_coefficients)


def solution(mesh):
    placed = (P(None, "gx", "gy"), P(None, "gx", "gy"), P("gx", "gy"), P("gx", "gy"), P(), P())
    return jax.shard_map(
        local,
        mesh=mesh,
        in_specs=placed,
        out_specs=(P(None, "gx", "gy"), P(), P()),
        check_vma=False,
    )
```

profile of v0, /device:TPU:1, one launch (start us, length us, event | category | flops | bytes accessed | tf_op | source)
XLA Modules:
  0.0 224.6 jit_solution(17356647873250402294)
XLA Ops:
  0.6 0.0 copy-start
  0.7 0.0 copy-start.2
  0.7 4.7 %fusion.13 = f32[1,128,256]{2,0,1:T(1,128)S(1)} fusion(bf16[64,128,256]{2,1,0:T(8,128)(2,1)} %param.7, f32[64]{0:T(128)} %param.10), kind=kOutput, calls=%fused_computation.18 | convolution fusion | flops 4194368 | bytes 4325632 | tf_op jit(solution)/shard_map/pxy,p->xy/dot_general | solution.py:36
  5.4 0.0 copy-done.7
  5.4 0.6 convert_reduce_fusion.1
  6.0 2.0 convert_reduce_fusion
  8.0 0.3 fusion.73
  8.3 4.9 %collective-permute-start = (bf16[64,64,256]{2,1,0:T(8,128)(2,1)S(1)}, bf16[64,64,256]{2,1,0:T(8,128)(2,1)S(1)}, u32[]{:S(2)}, u32[]{:S(2)}) collective-permute-start(bf16[64,64,256]{2,1,0:T(8,128)(2,1)S(1)} %get-tuple-element.11), channel_id=1, source_target_pairs={{0,16},{16,32},{32,48},{48,64},{64,80},{80,96},{96,112},{112,128},... | collective-permute-start | bytes 6291464 | tf_op jit(solution)/shard_map/ppermute | solution.py:17
  13.2 1.9 collective-permute-start.1
  15.2 21.0 %collective-permute-done = bf16[64,64,256]{2,1,0:T(8,128)(2,1)S(1)} collective-permute-done((bf16[64,64,256]{2,1,0:T(8,128)(2,1)S(1)}, bf16[64,64,256]{2,1,0:T(8,128)(2,1)S(1)}, u32[]{:S(2)}, u32[]{:S(2)}) %collective-permute-start) | collective-permute-done | bytes 2097184 | tf_op jit(solution)/shard_map/ppermute | solution.py:17
  36.2 4.4 %collective-permute-done.1 = bf16[64,64,256]{2,1,0:T(8,128)(2,1)S(1)} collective-permute-done((bf16[64,64,256]{2,1,0:T(8,128)(2,1)S(1)}, bf16[64,64,256]{2,1,0:T(8,128)(2,1)S(1)}, u32[]{:S(2)}, u32[]{:S(2)}) %collective-permute-start.1) | collective-permute-done | bytes 2097184 | tf_op jit(solution)/shard_map/ppermute | solution.py:20
  40.6 1.3 copy-done.6
  41.9 0.7 pad_maximum_fusion
  42.6 4.4 %fusion.72 = (bf16[64,256,64]{2,1,0:T(8,128)(2,1)}, bf16[64,256,64]{2,1,0:T(8,128)(2,1)}) fusion(bf16[64,256,256]{2,1,0:T(8,128)(2,1)S(1)} %pad_maximum_fusion), kind=kLoop, calls=%fused_computation.61 | loop fusion | bytes 8388608 | tf_op jit(solution)/shard_map/slice | solution.py:18
  47.1 3.5 %copy.15 = bf16[64,256,64]{1,2,0:T(8,128)(2,1)S(1)} copy(bf16[64,256,64]{2,1,0:T(8,128)(2,1)} %get-tuple-element.9) | data formatting | bytes 4194304 | tf_op jit(solution)/shard_map/slice | solution.py:18
  50.6 5.0 %collective-permute-start.2 = (bf16[64,256,64]{1,2,0:T(8,128)(2,1)S(1)}, bf16[64,256,64]{1,2,0:T(8,128)(2,1)}, u32[]{:S(2)}, u32[]{:S(2)}) collective-permute-start(bf16[64,256,64]{1,2,0:T(8,128)(2,1)S(1)} %copy.15), channel_id=1, source_target_pairs={{0,1},{1,2},{2,3},{3,4},{4,5},{5,6},{6,7},{7,8},{8,9},{9,10},{10,1... | collective-permute-start | bytes 6291464 | tf_op jit(solution)/shard_map/ppermute | solution.py:17
  55.6 4.8 %copy.16 = bf16[64,256,64]{1,2,0:T(8,128)(2,1)} copy(bf16[64,256,64]{2,1,0:T(8,128)(2,1)} %get-tuple-element.10) | data formatting | bytes 4194304 | tf_op jit(solution)/shard_map/slice | solution.py:20
  60.3 1.5 collective-permute-start.3
  61.8 0.0 copy-start.3
  61.8 2.7 %broadcast_multiply_fusion = bf16[64,128,256]{2,1,0:T(8,128)(2,1)S(1)} fusion(bf16[64,128,256]{2,1,0:T(8,128)(2,1)} %param.7, bf16[128,256]{1,0:T(8,128)(2,1)S(1)} %convert_element_type.43), kind=kLoop, calls=%fused_computation.26 | loop fusion | flops 2097152 | bytes 8454144 | tf_op jit(solution)/shard_map/mul | solution.py:58
  64.5 0.8 copy-done.3
  65.3 8.7 %fusion.32 = f32[64,64]{0,1:T(8,128)S(1)} fusion(bf16[64,128,256]{2,1,0:T(8,128)(2,1)S(1)} %copy-done.3, bf16[64,128,256]{2,1,0:T(8,128)(2,1)S(1)} %broadcast_multiply_fusion), kind=kOutput, calls=%fused_computation.28 | convolution fusion | flops 268435456 | bytes 8404992 | tf_op jit(solution)/shard_map/dot_general | solution.py:59
  74.0 4.4 %collective-permute-done.2 = bf16[64,256,64]{1,2,0:T(8,128)(2,1)} collective-permute-done((bf16[64,256,64]{1,2,0:T(8,128)(2,1)S(1)}, bf16[64,256,64]{1,2,0:T(8,128)(2,1)}, u32[]{:S(2)}, u32[]{:S(2)}) %collective-permute-start.2) | collective-permute-done | bytes 2097184 | tf_op jit(solution)/shard_map/ppermute | solution.py:17
  78.4 4.8 %copy.17 = bf16[64,256,64]{2,1,0:T(8,128)(2,1)} copy(bf16[64,256,64]{1,2,0:T(8,128)(2,1)} %collective-permute-done.2) | data formatting | bytes 4194304 | tf_op jit(solution)/shard_map/ppermute | solution.py:17
  83.2 5.7 %collective-permute-done.3 = bf16[64,256,64]{1,2,0:T(8,128)(2,1)} collective-permute-done((bf16[64,256,64]{1,2,0:T(8,128)(2,1)}, bf16[64,256,64]{1,2,0:T(8,128)(2,1)}, u32[]{:S(2)}, u32[]{:S(2)}) %collective-permute-start.3) | collective-permute-done | bytes 2097184 | tf_op jit(solution)/shard_map/ppermute | solution.py:20
  88.9 4.9 %copy.18 = bf16[64,256,64]{2,1,0:T(8,128)(2,1)} copy(bf16[64,256,64]{1,2,0:T(8,128)(2,1)} %collective-permute-done.3) | data formatting | bytes 4194304 | tf_op jit(solution)/shard_map/ppermute | solution.py:20
  93.8 16.0 %fusion.12 = bf16[64,128,256]{2,1,0:T(8,128)(2,1)} fusion(bf16[64,256,64]{2,1,0:T(8,128)(2,1)} %copy.18, bf16[64,64,256]{2,1,0:T(8,128)(2,1)} %copy-done.6, bf16[64,128,256]{2,1,0:T(8,128)(2,1)} %copy-done.1, bf16[64,64,256]{2,1,0:T(8,128)(2,1)S(1)} %copy-done.5, bf16[64,256,64]{2,1,0:T(8,128)(2,1)} %copy.17), kind=kOutput, calls=%fused_computation.17 | convolution fusion | flops 4371251200 | bytes 16777216 | tf_op jit(solution)/shard_map/kib,ia->kab/dot_general | solution.py:49
  109.8 12.2 %fusion.27 = f32[64,64]{1,0:T(8,128)S(1)} fusion(bf16[64,128,256]{2,1,0:T(8,128)(2,1)} %fusion.12, bf16[64,128,256]{2,1,0:T(8,128)(2,1)} %copy-done.1), kind=kOutput, calls=%fused_computation.27 | convolution fusion | flops 268435456 | bytes 8404992 | tf_op jit(solution)/shard_map/dot_general | solution.py:51
  122.1 99.0 %all-reduce = (f32[64,64]{1,0:T(8,128)S(1)}, f32[]{:T(128)}, f32[64]{0:T(128)S(1)}, f32[64,64]{0,1:T(8,128)S(1)}) all-reduce(f32[64,64]{1,0:T(8,128)S(1)} %fusion.27, f32[]{:T(128)} %get-tuple-element.13, f32[64]{0:T(128)S(1)} %get-tuple-element.7, f32[64,64]{0,1:T(8,128)S(1)} %fusion.32), channel_id=1, replica_groups=mesh['gx'=16,'gy'=16] {'gx','gy'}, use_global_device_ids=true, to_apply=%region_0.0 | all-reduce | flops 8257 | bytes 66056 | tf_op jit(solution)/shard_map/psum | solution.py:67
  221.8 0.8 convolution_bitcast_fusion.1
  222.6 1.4 fusion.38
  224.0 0.6 broadcast_multiply_fusion.1
  (15 shorter events, 0.0 us)
Async XLA Ops:
  0.6 221.2 %copy-start = (f32[64,64]{1,0:T(8,128)S(1)}, f32[64,64]{1,0:T(8,128)}, u32[]{:S(2)}) copy-start(f32[64,64]{1,0:T(8,128)} %param.11) | copy-start | bytes 49156
  0.6 4.7 %copy-start.8 = (f32[128,256]{1,0:T(8,128)S(1)}, f32[128,256]{1,0:T(8,128)}, u32[]{:S(2)}) copy-start(f32[128,256]{1,0:T(8,128)} %param.8) | copy-start | bytes 393220
  0.7 4.7 %copy-start.7 = (s32[128,256]{1,0:T(8,128)S(1)}, s32[128,256]{1,0:T(8,128)}, u32[]{:S(2)}) copy-start(s32[128,256]{1,0:T(8,128)} %param.9) | copy-start | bytes 393220
  0.7 5.3 %copy-start.2 = (bf16[64,128,256]{2,1,0:T(8,128)(2,1)S(1)}, bf16[64,128,256]{2,1,0:T(8,128)(2,1)}, u32[]{:S(2)}) copy-start(bf16[64,128,256]{2,1,0:T(8,128)(2,1)} %param.6) | copy-start | bytes 12582916
  8.0 32.6 %copy-start.1 = (bf16[64,128,256]{2,1,0:T(8,128)(2,1)}, bf16[64,128,256]{2,1,0:T(8,128)(2,1)S(1)}, u32[]{:S(2)}) copy-start(bf16[64,128,256]{2,1,0:T(8,128)(2,1)S(1)} %get-tuple-element.8) | copy-start | bytes 12582916
  8.3 27.9 %collective-permute-start = (bf16[64,64,256]{2,1,0:T(8,128)(2,1)S(1)}, bf16[64,64,256]{2,1,0:T(8,128)(2,1)S(1)}, u32[]{:S(2)}, u32[]{:S(2)}) collective-permute-start(bf16[64,64,256]{2,1,0:T(8,128)(2,1)S(1)} %get-tuple-element.11), channel_id=1, source_target_pairs={{0,16},{16,32},{32,48},{48,64},{64,80},{80,96},{96,112},{112,128},... | collective-permute-start | bytes 6291464 | tf_op jit(solution)/shard_map/ppermute | solution.py:17
  13.2 27.4 %collective-permute-start.1 = (bf16[64,64,256]{2,1,0:T(8,128)(2,1)S(1)}, bf16[64,64,256]{2,1,0:T(8,128)(2,1)S(1)}, u32[]{:S(2)}, u32[]{:S(2)}) collective-permute-start(bf16[64,64,256]{2,1,0:T(8,128)(2,1)S(1)} %get-tuple-element.12), channel_id=1, source_target_pairs={{16,0},{32,16},{48,32},{64,48},{80,64},{96,80},{112,96},{128,112},... | collective-permute-start | bytes 6291464 | tf_op jit(solution)/shard_map/ppermute | solution.py:20
  36.2 4.4 %copy-start.4 = (bf16[64,64,256]{2,1,0:T(8,128)(2,1)}, bf16[64,64,256]{2,1,0:T(8,128)(2,1)S(1)}, u32[]{:S(2)}) copy-start(bf16[64,64,256]{2,1,0:T(8,128)(2,1)S(1)} %collective-permute-done) | copy-start | bytes 6291460
  40.6 1.3 copy-start.6
  50.6 27.8 %collective-permute-start.2 = (bf16[64,256,64]{1,2,0:T(8,128)(2,1)S(1)}, bf16[64,256,64]{1,2,0:T(8,128)(2,1)}, u32[]{:S(2)}, u32[]{:S(2)}) collective-permute-start(bf16[64,256,64]{1,2,0:T(8,128)(2,1)S(1)} %copy.15), channel_id=1, source_target_pairs={{0,1},{1,2},{2,3},{3,4},{4,5},{5,6},{6,7},{7,8},{8,9},{9,10},{10,1... | collective-permute-start | bytes 6291464 | tf_op jit(solution)/shard_map/ppermute | solution.py:17
  60.3 28.6 %collective-permute-start.3 = (bf16[64,256,64]{1,2,0:T(8,128)(2,1)}, bf16[64,256,64]{1,2,0:T(8,128)(2,1)}, u32[]{:S(2)}, u32[]{:S(2)}) collective-permute-start(bf16[64,256,64]{1,2,0:T(8,128)(2,1)} %copy.16), channel_id=1, source_target_pairs={{1,0},{2,1},{3,2},{4,3},{5,4},{6,5},{7,6},{8,7},{9,8},{10,9},{11,1... | collective-permute-start | bytes 6291464 | tf_op jit(solution)/shard_map/ppermute | solution.py:20
  61.8 3.5 %copy-start.3 = (bf16[64,128,256]{2,1,0:T(8,128)(2,1)S(1)}, bf16[64,128,256]{2,1,0:T(8,128)(2,1)}, u32[]{:S(2)}) copy-start(bf16[64,128,256]{2,1,0:T(8,128)(2,1)} %param.6) | copy-start | bytes 12582916
  83.2 10.6 %copy-start.5 = (bf16[64,64,256]{2,1,0:T(8,128)(2,1)S(1)}, bf16[64,64,256]{2,1,0:T(8,128)(2,1)}, u32[]{:S(2)}) copy-start(bf16[64,64,256]{2,1,0:T(8,128)(2,1)} %copy-done.4) | copy-start | bytes 6291460
  109.8 112.7 %copy-start.9 = (f32[64]{0:T(128)S(1)}, f32[64]{0:T(128)}, u32[]{:S(2)}) copy-start(f32[64]{0:T(128)} %param.10) | copy-start | bytes 772
where the time goes:
time: 225 us
  blocking collectives  99 us (44%)
  matrix products  43.8 us (19%)
  waiting for transfers between devices  35.6 us (16%)
  local copies, waits for them, and re-layouts  24.8 us (11%)
  starting transfers between devices  13.3 us (6%)
  other arithmetic  6.59 us (3%)
    psum x1, blocking collectives, local(): lax.psum((products, cross_part, moment_part, land_part), ('gx', 'gy'))  99 us
    ppermute x2, waiting for transfers between devices, padded_2(): lax.ppermute(lax.slice_in_dim(block, block.shape[dim] - width, None, axis...  25.4 us
    dot_general x1, matrix products, local(): jnp.einsum('kib,ia->kab', across, band_first, preferred_element_type=jnp....  16 us
    dot_general x1, matrix products, local(): lax.dot_general(moments.reshape(channels, -1), smoothed.reshape(channels,...  12.2 us
    ppermute x2, waiting for transfers between devices, padded_2(): lax.ppermute(lax.slice_in_dim(block, 0, width, axis=dim), axis, backward)  10.1 us
    ppermute x2, starting transfers between devices, padded_2(): lax.ppermute(lax.slice_in_dim(block, block.shape[dim] - width, None, axis...  9.9 us
    dot_general x1, matrix products, local(): lax.dot_general(flat_inst, flat_reg, (((1,), (1,)), ((), ())), preferred_...  8.73 us
    slice x3, local copies, waits for them, and re-layouts, padded_2(): lax.slice_in_dim(block, block.shape[dim] - width, None, axis=dim)  8.26 us
  transfers between devices with their start and end apart: 4, of which 4 were waited for; matrix products, arithmetic and copies ran while one was open for 9% of the time, Pallas kernels for 0%

commit v1 on v0

v1 whole, which is shorter than its diff:
```python
import functools

import jax
import jax.numpy as jnp
from jax import lax
from jax.experimental import pallas as pl
from jax.experimental.pallas import tpu as pltpu
from jax.sharding import PartitionSpec as P

B = 64
step_rate = 0.05
MESH = pl.DeviceIdType.MESH
F32 = jnp.float32
BF16 = jnp.bfloat16
CH = 8
GROUP = 16
SUB = 16


def iota(shape, dim):
    return lax.broadcasted_iota(jnp.int32, shape, dim)


def dot(a, b):
    return lax.dot_general(a, b, (((1,), (0,)), ((), ())), preferred_element_type=F32)


def dot_t(a, b):
    return lax.dot_general(a, b, (((1,), (1,)), ((), ())), preferred_element_type=F32)


def hat(distance):
    return jnp.maximum(B + 1 - jnp.abs(distance), 0).astype(F32).astype(BF16)


def kernel(
    nx,
    ny,
    inst_h,
    reg_h,
    outcome_h,
    land_h,
    coef_s,
    coef_v,
    wgt_v,
    s_h,
    hac_v,
    new_v,
    inst,
    reg,
    outcome,
    land,
    coefs,
    weighted,
    land_half,
    mom,
    send_l,
    send_r,
    y_l,
    y_r,
    rows_sm,
    sm,
    w_top,
    w_bot,
    w_col,
    acc,
    cov,
    jac,
    sums,
    part,
    got1,
    sum1,
    got2,
    sum2,
    got3,
    in_sem,
    reg_sem,
    inst_sem,
    yl_send,
    yl_recv,
    yr_send,
    yr_recv,
    zt_send,
    zt_recv,
    zb_send,
    zb_recv,
    out_sem,
    ar_send,
    ar_recv,
):
    gx = lax.axis_index("gx")
    gy = lax.axis_index("gy")
    channels, rows, cols = inst.shape
    half = rows // 2
    n_chunks = channels // CH
    n_groups = channels // GROUP
    n_sub = rows // SUB
    reg_rows = rows // 4

    def outcome_copy():
        return pltpu.make_async_copy(outcome_h, outcome, in_sem.at[0])

    def land_copy():
        return pltpu.make_async_copy(land_h, land, in_sem.at[1])

    def reg_copy(r):
        at = pl.ds(pl.multiple_of(r * reg_rows, reg_rows), reg_rows)
        return pltpu.make_async_copy(reg_h.at[:, at, :], reg.at[:, at, :], reg_sem.at[r])

    def inst_copy(g):
        at = pl.ds(g * GROUP, GROUP)
        return pltpu.make_async_copy(inst_h.at[at], inst.at[at], inst_sem.at[g])

    outcome_copy().start()
    land_copy().start()
    for r in range(4):
        reg_copy(r).start()
    for g in range(n_groups):
        inst_copy(g).start()

    barrier = pltpu.get_barrier_semaphore()

    def greet_x(g, carry):
        @pl.when(g != gx)
        def _():
            pl.semaphore_signal(barrier, inc=1, device_id=(g, gy), device_id_type=MESH)

        return carry

    def greet_y(g, carry):
        @pl.when(g != gy)
        def _():
            pl.semaphore_signal(barrier, inc=1, device_id=(gx, g), device_id_type=MESH)

        return carry

    lax.fori_loop(0, nx, greet_x, 0)
    lax.fori_loop(0, ny, greet_y, 0)

    for p in range(channels):
        coefs[p : p + 1, :] = jnp.full((1, cols), coef_s[p], F32)
    coefs[...] = coefs[...].astype(BF16).astype(F32)

    src = iota((cols, cols), 0)
    dst = iota((cols, cols), 1)
    own = hat(src - dst)
    w_top[0:cols, :] = own
    w_bot[0:cols, :] = own
    low = src % half
    side = jnp.where(src < 2 * half, low - half, low + cols)
    ramp = jnp.maximum(B + 1 - jnp.abs(side - dst), 0).astype(F32)
    is_top = (src // half) % 2 == 0
    w_top[cols : 2 * cols, :] = jnp.where(is_top, ramp, 0.0).astype(BF16)
    w_bot[cols : 2 * cols, :] = jnp.where(is_top, 0.0, ramp).astype(BF16)
    w_col[...] = hat(iota((rows, 2 * rows), 1) - half - iota((rows, 2 * rows), 0))

    @pl.when(gy == 0)
    def _():
        y_l[...] = jnp.zeros_like(y_l)

    @pl.when(gy == ny - 1)
    def _():
        y_r[...] = jnp.zeros_like(y_r)

    def clear(start):
        def body(k, carry):
            rows_sm[k, start : start + half, :] = jnp.zeros((half, cols), BF16)
            return carry

        lax.fori_loop(0, channels, body, 0)

    @pl.when(gx == 0)
    def _():
        clear(0)

    @pl.when(gx == nx - 1)
    def _():
        clear(rows + half)

    outcome_copy().wait()
    land_copy().wait()

    def residuals(r, carry):
        reg_copy(r).wait()
        at = pl.ds(pl.multiple_of(r * reg_rows, reg_rows), reg_rows)

        def add(q, total):
            for u in range(8):
                p = q * 8 + u
                total = total + reg[p, at, :].astype(F32) * coefs[pl.ds(p, 1), :]
            return total

        fitted = lax.fori_loop(0, channels // 8, add, jnp.zeros((reg_rows, cols), F32))
        land_float = land[at, :].astype(F32)
        weighted[at, :] = land_float * (outcome[at, :] - fitted)
        land_half[at, :] = land_float.astype(BF16)
        return carry

    lax.fori_loop(0, 4, residuals, 0)

    pl.semaphore_wait(barrier, nx - 1 + ny - 1)

    def to_left(c):
        at = pl.ds(c * CH, CH)
        return pltpu.make_async_remote_copy(
            src_ref=send_l.at[at],
            dst_ref=y_r.at[at],
            send_sem=yl_send.at[c],
            recv_sem=yr_recv.at[c],
            device_id=(gx, gy - 1),
            device_id_type=MESH,
        )

    def to_right(c):
        at = pl.ds(c * CH, CH)
        return pltpu.make_async_remote_copy(
            src_ref=send_r.at[at],
            dst_ref=y_l.at[at],
            send_sem=yr_send.at[c],
            recv_sem=yl_recv.at[c],
            device_id=(gx, gy + 1),
            device_id_type=MESH,
        )

    def to_upper(c):
        at = pl.ds(c * CH, CH)
        return pltpu.make_async_remote_copy(
            src_ref=rows_sm.at[at, half : 2 * half, :],
            dst_ref=rows_sm.at[at, 3 * half : 4 * half, :],
            send_sem=zt_send.at[c],
            recv_sem=zb_recv.at[c],
            device_id=(gx - 1, gy),
            device_id_type=MESH,
        )

    def to_lower(c):
        at = pl.ds(c * CH, CH)
        return pltpu.make_async_remote_copy(
            src_ref=rows_sm.at[at, 2 * half : 3 * half, :],
            dst_ref=rows_sm.at[at, 0:half, :],
            send_sem=zb_send.at[c],
            recv_sem=zt_recv.at[c],
            device_id=(gx + 1, gy),
            device_id_type=MESH,
        )

    has_left, has_right = gy > 0, gy < ny - 1
    has_upper, has_lower = gx > 0, gx < nx - 1

    first_lanes = iota((SUB, 128), 1) < B

    def moments(c, carry):
        @pl.when(c % (GROUP // CH) == 0)
        def _():
            inst_copy(c // (GROUP // CH)).wait()

        def channel(u, inner):
            k = c * CH + u
            for r in range(0, half, SUB):
                upper, lower = slice(r, r + SUB), slice(half + r, half + r + SUB)
                top = inst[k, upper, :].astype(F32) * weighted[upper, :]
                bot = inst[k, lower, :].astype(F32) * weighted[lower, :]
                mom[k, upper, :] = top.astype(BF16)
                mom[k, lower, :] = bot.astype(BF16)
                left = jnp.where(first_lanes, top[:, :128], pltpu.roll(bot[:, :128], B, 1))
                right = jnp.where(first_lanes, pltpu.roll(top[:, cols - 128 :], B, 1), bot[:, cols - 128 :])
                send_l[k, upper, :] = left.astype(BF16)
                send_r[k, upper, :] = right.astype(BF16)
            return inner

        lax.fori_loop(0, CH, channel, 0)

        @pl.when(has_left)
        def _():
            to_left(c).start()

        @pl.when(has_right)
        def _():
            to_right(c).start()

        return carry

    lax.fori_loop(0, n_chunks, moments, 0)

    lanes = iota((1, SUB, GROUP * SUB), 2)
    diagonal = lanes % SUB == iota((1, SUB, GROUP * SUB), 1)

    def fold(total, g):
        kept = jnp.where(diagonal, total.reshape(channels, SUB, GROUP * SUB), 0.0)
        kept = jnp.sum(kept, axis=1)
        pick = iota((GROUP * SUB, 128), 0) // SUB + g * GROUP == iota((GROUP * SUB, 128), 1)
        return lax.dot_general(
            kept,
            pick.astype(F32),
            (((1,), (0,)), ((), ())),
            precision=lax.Precision.HIGHEST,
            preferred_element_type=F32,
        )

    def block(ref, first, count, b):
        at = pl.ds(pl.multiple_of(b * SUB, SUB), SUB)
        return ref[pl.ds(first, count), at, :]

    def jac_group(g):
        acc[...] = jnp.zeros_like(acc)

        def step(b, carry):
            land_b = land_half[pl.ds(pl.multiple_of(b * SUB, SUB), SUB), :]
            lhs = (block(inst, 0, channels, b) * land_b[None]).reshape(channels * SUB, cols)
            rhs = block(reg, g * GROUP, GROUP, b).reshape(GROUP * SUB, cols)
            acc[...] += dot_t(lhs, rhs)
            return carry

        lax.fori_loop(0, n_sub, step, 0)
        jac[...] += fold(acc[...], g)

    def cov_group(g):
        acc[...] = jnp.zeros_like(acc)

        def step(b, carry):
            lhs = block(mom, 0, channels, b).reshape(channels * SUB, cols)
            rhs = block(sm, g * GROUP, GROUP, b).reshape(GROUP * SUB, cols)
            acc[...] += dot_t(lhs, rhs)
            return carry

        lax.fori_loop(0, n_sub, step, 0)
        cov[...] += fold(acc[...], g)

    def sum_group(g):
        for u in range(0, GROUP, 8):
            at = pl.ds(pl.multiple_of(g * GROUP + u, 8), 8)
            sums[at, :] = jnp.sum(mom[at].astype(F32), axis=1)

    cov[...] = jnp.zeros_like(cov)
    jac[...] = jnp.zeros_like(jac)

    def out_copy(c):
        at = pl.ds(c * CH, CH)
        return pltpu.make_async_copy(sm.at[at], s_h.at[at], out_sem.at[c])

    def smooth_rows(c):
        @pl.when(has_left)
        def _():
            to_right(c).wait_recv()

        @pl.when(has_right)
        def _():
            to_left(c).wait_recv()

        at = pl.ds(c * CH, CH)
        edges = jnp.concatenate(
            [y_l[at].reshape(CH * half, 128), y_r[at].reshape(CH * half, 128)], axis=1
        )
        for start, weights in ((0, w_top), (half, w_bot)):
            here = mom[at, start : start + half, :].reshape(CH * half, cols)
            total = dot(jnp.concatenate([here, edges], axis=1), weights[...])
            rows_sm[at, half + start : 2 * half + start, :] = (
                (total * (1.0 / (B + 1))).astype(BF16).reshape(CH, half, cols)
            )

        @pl.when(has_upper)
        def _():
            to_upper(c).start()

        @pl.when(has_lower)
        def _():
            to_lower(c).start()

    def smooth_columns(c):
        @pl.when(has_upper)
        def _():
            to_lower(c).wait_recv()

        @pl.when(has_lower)
        def _():
            to_upper(c).wait_recv()

        def channel(u, inner):
            k = c * CH + u
            total = dot(w_col[...], rows_sm[k])
            sm[k] = (total * (1.0 / (B + 1) ** 2)).astype(BF16)
            return inner

        lax.fori_loop(0, CH, channel, 0)
        out_copy(c).start()

    def pipeline(t, carry):
        @pl.when(t < n_chunks)
        def _():
            smooth_rows(t)

        @pl.when(t < n_groups)
        def _():
            jac_group(t)
            sum_group(t)

        @pl.when(t >= 1)
        def _():
            smooth_columns(t - 1)

        @pl.when(jnp.logical_and(t >= 1, t % (GROUP // CH) == 0))
        def _():
            cov_group(t // (GROUP // CH) - 1)

        return carry

    lax.fori_loop(0, n_chunks + 1, pipeline, 0)

    pieces = channels // 8
    own_pieces = 2 * pieces // nx
    count = jnp.sum(jnp.sum(land_half[...].astype(F32), axis=0, keepdims=True), axis=1, keepdims=True)
    columns = jnp.sum(sums[...], axis=1, keepdims=True)
    right_half = iota((channels, 128), 1) >= channels
    as_row = jnp.sum(
        jnp.where(iota((channels, 128), 1) - channels == iota((channels, 128), 0), columns, 0.0), axis=0, keepdims=True
    )
    part[0:pieces] = jnp.where(right_half, count, cov[...]).reshape(pieces, 8, 128)
    part[pieces : 2 * pieces] = jnp.where(right_half, as_row, jac[...]).reshape(pieces, 8, 128)

    def exchange(number, peers, me, copy, landed, sent):
        def send(g, carry):
            @pl.when(g != me)
            def _():
                copy(g).start()

            return carry

        lax.fori_loop(0, peers, send, 0)
        pltpu.make_async_copy(landed, landed, ar_recv.at[number]).wait()
        pltpu.make_async_copy(sent, sent, ar_send.at[number]).wait()

    def own(g):
        return pl.ds(g * own_pieces, own_pieces)

    def scatter(g):
        return pltpu.make_async_remote_copy(
            src_ref=part.at[own(g)],
            dst_ref=got1.at[gx],
            send_sem=ar_send.at[0],
            recv_sem=ar_recv.at[0],
            device_id=(g, gy),
            device_id_type=MESH,
        )

    def across(g):
        return pltpu.make_async_remote_copy(
            src_ref=sum1,
            dst_ref=got2.at[gy],
            send_sem=ar_send.at[1],
            recv_sem=ar_recv.at[1],
            device_id=(gx, g),
            device_id_type=MESH,
        )

    def gather(g):
        return pltpu.make_async_remote_copy(
            src_ref=sum2,
            dst_ref=got3.at[own(gx)],
            send_sem=ar_send.at[2],
            recv_sem=ar_recv.at[2],
            device_id=(g, gy),
            device_id_type=MESH,
        )

    got1[gx] = part[own(gx)]
    exchange(0, nx, gx, scatter, got1.at[0 : nx - 1], got1.at[0 : nx - 1])
    sum1[...] = jnp.sum(got1[...], axis=0)
    got2[gy] = sum1[...]
    exchange(1, ny, gy, across, got2.at[0 : ny - 1], got2.at[0 : ny - 1])
    sum2[...] = jnp.sum(got2[...], axis=0)
    got3[own(gx)] = sum2[...]
    rest = got3.at[0 : (nx - 1) * own_pieces]
    exchange(2, nx, gx, gather, rest, rest)

    first = got3[0:pieces].reshape(channels, 128)
    second = got3[pieces : 2 * pieces].reshape(channels, 128)
    land_total = first[:, channels : channels + 1]
    hac_v[...] = first[:, :channels] * ((B + 1) / land_total)
    mean = second[0:1, channels:] / land_total[0:1, :]
    weighed = jnp.sum(wgt_v[...] * mean, axis=1, keepdims=True)
    jacobian = -second[:, :channels] / land_total
    gradient = 2.0 * jnp.sum(jacobian * weighed, axis=0, keepdims=True)
    new_v[...] = coef_v[...] - step_rate * gradient

    def drain(c, carry):
        out_copy(c).wait()

        @pl.when(has_left)
        def _():
            to_left(c).wait_send()

        @pl.when(has_right)
        def _():
            to_right(c).wait_send()

        @pl.when(has_upper)
        def _():
            to_upper(c).wait_send()

        @pl.when(has_lower)
        def _():
            to_lower(c).wait_send()

        return carry

    lax.fori_loop(0, n_chunks, drain, 0)


def local(nx, ny, instruments, regressors, outcome, land_mask, coefficients, weighting):
    channels, rows, cols = instruments.shape
    n_chunks = channels // CH
    pieces = channels // 8
    own = 2 * pieces // nx
    any_spec = pl.BlockSpec(memory_space=pl.ANY)
    vmem_spec = pl.BlockSpec(memory_space=pltpu.VMEM)
    dma = pltpu.SemaphoreType.DMA
    smoothed, hac_cov, new_coefficients = pl.pallas_call(
        functools.partial(kernel, nx, ny),
        out_shape=(
            jax.ShapeDtypeStruct((channels, rows, cols), BF16),
            jax.ShapeDtypeStruct((channels, channels), F32),
            jax.ShapeDtypeStruct((1, channels), F32),
        ),
        in_specs=[any_spec] * 4 + [pl.BlockSpec(memory_space=pltpu.SMEM), vmem_spec, vmem_spec],
        out_specs=(any_spec, vmem_spec, vmem_spec),
        scratch_shapes=[
            pltpu.VMEM((channels, rows, cols), BF16),
            pltpu.VMEM((channels, rows, cols), BF16),
            pltpu.VMEM((rows, cols), F32),
            pltpu.VMEM((rows, cols), jnp.int32),
            pltpu.VMEM((channels, cols), F32),
            pltpu.VMEM((rows, cols), F32),
            pltpu.VMEM((rows, cols), BF16),
            pltpu.VMEM((channels, rows, cols), BF16),
            pltpu.VMEM((channels, rows // 2, 128), BF16),
            pltpu.VMEM((channels, rows // 2, 128), BF16),
            pltpu.VMEM((channels, rows // 2, 128), BF16),
            pltpu.VMEM((channels, rows // 2, 128), BF16),
            pltpu.VMEM((channels, 2 * rows, cols), BF16),
            pltpu.VMEM((channels, rows, cols), BF16),
            pltpu.VMEM((2 * cols, cols), BF16),
            pltpu.VMEM((2 * cols, cols), BF16),
            pltpu.VMEM((rows, 2 * rows), BF16),
            pltpu.VMEM((channels * SUB, GROUP * SUB), F32),
            pltpu.VMEM((channels, 128), F32),
            pltpu.VMEM((channels, 128), F32),
            pltpu.VMEM((channels, cols), F32),
            pltpu.VMEM((2 * pieces, 8, 128), F32),
            pltpu.VMEM((nx, own, 8, 128), F32),
            pltpu.VMEM((own, 8, 128), F32),
            pltpu.VMEM((ny, own, 8, 128), F32),
            pltpu.VMEM((own, 8, 128), F32),
            pltpu.VMEM((2 * pieces, 8, 128), F32),
            dma((2,)),
            dma((4,)),
            dma((channels // GROUP,)),
        ]
        + [dma((n_chunks,))] * 9
        + [dma((3,)), dma((3,))],
        compiler_params=pltpu.CompilerParams(
            collective_id=0, has_side_effects=True, vmem_limit_bytes=48 * 1024 * 1024
        ),
        cost_estimate=pl.CostEstimate(flops=5 * 10**9, bytes_accessed=13 * 2**20, transcendentals=0),
    )(
        instruments,
        regressors,
        outcome,
        land_mask,
        coefficients,
        coefficients.reshape(1, channels),
        weighting,
    )
    return smoothed, hac_cov, new_coefficients.reshape(channels)


def solution(mesh):
    placed = (P(None, "gx", "gy"), P(None, "gx", "gy"), P("gx", "gy"), P("gx", "gy"), P(), P())
    return jax.shard_map(
        functools.partial(local, mesh.shape["gx"], mesh.shape["gy"]),
        mesh=mesh,
        in_specs=placed,
        out_specs=(P(None, "gx", "gy"), P(), P()),
        check_vma=False,
    )
```

time: 225 us -> 88.9 us (0.40)
  blocking collectives: 99 us -> 0 us
  Pallas kernels: 0 us -> 81.7 us
  matrix products: 43.8 us -> 0 us
  waiting for transfers between devices: 35.6 us -> 0 us
  local copies, waits for them, and re-layouts: 24.8 us -> 6.35 us
  starting transfers between devices: 13.3 us -> 0 us
  other arithmetic: 6.59 us -> 0 us
    psum x1 -> x0, blocking collectives: 99 us -> none  [local(): lax.psum((products, cross_part, moment_part, land_part), ('gx', 'gy'))]
    pallas_call x0 -> x1, Pallas kernels: none -> 81.7 us  [local(): pl.pallas_call(functools.partial(kernel, nx, ny), out_shape=(jax.ShapeDty...]
    dot_general x6 -> x0, matrix products: 43.8 us -> none  [the longest x1 16 us: local(): jnp.einsum('kib,ia->kab', across, band_first, preferred_element_type=jnp....]
    ppermute x4 -> x0, waiting for transfers between devices: 35.6 us -> none  [the longest x2 25.4 us: padded_2(): lax.ppermute(lax.slice_in_dim(block, block.shape[dim] - width, None, axis...]
    ppermute x4 -> x0, starting transfers between devices: 13.3 us -> none  [the longest x2 9.9 us: padded_2(): lax.ppermute(lax.slice_in_dim(block, block.shape[dim] - width, None, axis...]
    slice x4 -> x0, local copies, waits for them, and re-layouts: 13 us -> none  [the longest x3 8.26 us: padded_2(): lax.slice_in_dim(block, block.shape[dim] - width, None, axis=dim)]
    ppermute x2 -> x0, local copies, waits for them, and re-layouts: 9.67 us -> none  [the longest x1 4.88 us: padded_2(): lax.ppermute(lax.slice_in_dim(block, 0, width, axis=dim), axis, backward)]
    unnamed x20 -> x11, local copies, waits for them, and re-layouts: 2.15 us -> 6.35 us
  transfers between devices with their start and end apart: 4 -> 0, of which waited for: 4 -> 0; matrix products, arithmetic and copies ran while one was open for 9% -> 0% of each run, Pallas kernels for 0% -> 0%
where the time goes in v1:
time: 88.9 us; the launch traced here: 88.7 us
  Pallas kernels  81.7 us (92%)
  local copies, waits for them, and re-layouts  6.35 us (7%)
    pallas_call x1, Pallas kernels, local(): pl.pallas_call(functools.partial(kernel, nx, ny), out_shape=(jax.ShapeDty...  81.7 us
    unnamed x11, local copies, waits for them, and re-layouts  6.35 us

profile of v1, /device:TPU:1, one launch (start us, length us, event | category | flops | bytes accessed | tf_op | source)
XLA Modules:
  0.0 88.7 jit_solution(16758283641632821689)
XLA Ops:
  0.6 0.0 copy-start
  0.6 0.9 %copy-done = f32[128,256]{1,0:T(8,128)S(1)} copy-done((f32[128,256]{1,0:T(8,128)S(1)}, f32[128,256]{1,0:T(8,128)}, u32[]{:S(2)}) %copy-start) | copy-done | bytes 131096
  1.5 0.0 copy-start.1
  1.5 0.9 %copy-done.1 = s32[128,256]{1,0:T(8,128)S(1)} copy-done((s32[128,256]{1,0:T(8,128)S(1)}, s32[128,256]{1,0:T(8,128)}, u32[]{:S(2)}) %copy-start.1) | copy-done | bytes 131096
  2.4 0.0 copy-start.2
  2.4 0.8 copy-done.2
  3.2 0.0 copy-start.3
  3.2 0.7 copy-done.3
  3.9 81.7 %shard_map.85 = (bf16[64,128,256]{2,1,0:T(8,128)(2,1)S(1)}, f32[64,64]{1,0:T(8,128)S(1)}, f32[1,64]{1,0:T(1,128)S(1)}) custom-call(bf16[64,128,256]{2,1,0:T(8,128)(2,1)} %inst_h.1, bf16[64,128,256]{2,1,0:T(8,128)(2,1)} %reg_h.1, f32[128,256]{1,0:T(8,128)S(1)} %copy-done, s32[128,256]{1,0:T(8,128)S(1)} %copy-done.1, f32[64]{0:T(128)S(1)} %copy-done.3, ...), custom_call_target="tpu_custom_call" | custom-call | flops 5000000000 | bytes 13631488 | tf_op jit(solution)/shard_map/pallas_call | solution.py:517
  85.6 2.0 %copy.12 = bf16[64,128,256]{2,1,0:T(8,128)(2,1)} copy(bf16[64,128,256]{2,1,0:T(8,128)(2,1)S(1)} %get-tuple-element.12) | data formatting | bytes 8388608
  87.6 0.6 copy.13
  88.2 0.5 copy.14
Async XLA Ops:
  0.6 0.9 %copy-start = (f32[128,256]{1,0:T(8,128)S(1)}, f32[128,256]{1,0:T(8,128)}, u32[]{:S(2)}) copy-start(f32[128,256]{1,0:T(8,128)} %outcome_h.1) | copy-start | bytes 393220
  1.5 0.9 %copy-start.1 = (s32[128,256]{1,0:T(8,128)S(1)}, s32[128,256]{1,0:T(8,128)}, u32[]{:S(2)}) copy-start(s32[128,256]{1,0:T(8,128)} %land_h.1) | copy-start | bytes 393220
  2.4 0.8 copy-start.2
  3.2 0.7 copy-start.3

commit v2 on v1

v2 whole, which is shorter than its diff:
```python
import functools

import jax
import jax.numpy as jnp
from jax import lax
from jax.experimental import pallas as pl
from jax.experimental.pallas import tpu as pltpu
from jax.sharding import PartitionSpec as P

B = 64
step_rate = 0.05
MESH = pl.DeviceIdType.MESH
F32 = jnp.float32
BF16 = jnp.bfloat16
CH = 8
SUB = 8
LAG = 1
COV_BLOCKS = ((0, 32), (32, 16), (48, 16))
JAC_BLOCK = 32
TAIL = 32


def iota(shape, dim):
    return lax.broadcasted_iota(jnp.int32, shape, dim)


def dot(a, b):
    return lax.dot_general(a, b, (((1,), (0,)), ((), ())), preferred_element_type=F32)


def dot_t(a, b):
    return lax.dot_general(a, b, (((1,), (1,)), ((), ())), preferred_element_type=F32)


def wide(ref, *at):
    return jnp.concatenate([ref[(0, *at)], ref[(1, *at)]], axis=-1)


def put_wide(ref, value):
    ref[0] = value[:, :128]
    ref[1] = value[:, 128:]


def hat(distance):
    return jnp.maximum(B + 1 - jnp.abs(distance), 0).astype(F32).astype(BF16)


def kernel(
    nx,
    ny,
    inst_h,
    reg_h,
    outcome_h,
    land_h,
    coef_h,
    sm,
    total_v,
    tail_v,
    inst,
    reg,
    outcome,
    land,
    coef_s,
    coefs,
    weighted,
    land_float,
    mom,
    inst_b,
    reg_b,
    send_l,
    send_r,
    y_l,
    y_r,
    rows_sm,
    sm_b,
    w_top,
    w_bot,
    w_col,
    acc_cov,
    acc_jac,
    cov,
    cov_tail,
    jac,
    sums,
    part,
    got1,
    sum1,
    got2,
    sum2,
    got3,
    tile,
    got4,
    sum4,
    got5,
    in_sem,
    reg_sem,
    inst_sem,
    yl_send,
    yl_recv,
    yr_send,
    yr_recv,
    zt_send,
    zt_recv,
    zb_send,
    zb_recv,
    ar_send,
    ar_recv,
):
    gx = lax.axis_index("gx")
    gy = lax.axis_index("gy")
    channels, rows, cols = inst.shape
    half = rows // 2
    n_chunks = channels // CH
    reg_rows = rows // 4
    blocks = rows // SUB

    def outcome_copy():
        return pltpu.make_async_copy(outcome_h, outcome, in_sem.at[0])

    def land_copy():
        return pltpu.make_async_copy(land_h, land, in_sem.at[1])

    def coef_copy():
        return pltpu.make_async_copy(coef_h, coef_s, in_sem.at[2])

    def reg_copy(r):
        at = pl.ds(pl.multiple_of(r * reg_rows, reg_rows), reg_rows)
        return pltpu.make_async_copy(reg_h.at[:, at, :], reg.at[:, at, :], reg_sem.at[r])

    def inst_copy(c):
        at = pl.ds(c * CH, CH)
        return pltpu.make_async_copy(inst_h.at[at], inst.at[at], inst_sem.at[c])

    coef_copy().start()
    reg_copy(0).start()
    outcome_copy().start()
    land_copy().start()
    for r in range(1, 4):
        reg_copy(r).start()
    for c in range(n_chunks):
        inst_copy(c).start()

    barrier = pltpu.get_barrier_semaphore()

    def greet_x(o, carry):
        pl.semaphore_signal(barrier, inc=1, device_id=((gx + o) % nx, gy), device_id_type=MESH)
        return carry

    def greet_y(o, carry):
        pl.semaphore_signal(barrier, inc=1, device_id=(gx, (gy + o) % ny), device_id_type=MESH)
        return carry

    lax.fori_loop(1, nx, greet_x, 0)
    lax.fori_loop(1, ny, greet_y, 0)

    src = iota((cols, cols), 0)
    dst = iota((cols, cols), 1)
    own_band = hat(src - dst)
    low = src % half
    side = jnp.where(src < 2 * half, low - half, low + cols)
    ramp = jnp.maximum(B + 1 - jnp.abs(side - dst), 0).astype(F32)
    is_top = (src // half) % 2 == 0
    put_wide(w_top, jnp.concatenate([own_band, jnp.where(is_top, ramp, 0.0).astype(BF16)], axis=0))
    put_wide(w_bot, jnp.concatenate([own_band, jnp.where(is_top, 0.0, ramp).astype(BF16)], axis=0))
    put_wide(w_col, hat(iota((rows, 2 * rows), 1) - half - iota((rows, 2 * rows), 0)))

    @pl.when(gy == 0)
    def _():
        y_l[...] = jnp.zeros_like(y_l)

    @pl.when(gy == ny - 1)
    def _():
        y_r[...] = jnp.zeros_like(y_r)

    def clear(start):
        def body(k, carry):
            rows_sm[:, k, start : start + half, :] = jnp.zeros((2, half, 128), BF16)
            return carry

        lax.fori_loop(0, channels, body, 0)

    @pl.when(gx == 0)
    def _():
        clear(0)

    @pl.when(gx == nx - 1)
    def _():
        clear(rows + half)

    cov[...] = jnp.zeros_like(cov)
    cov_tail[...] = jnp.zeros_like(cov_tail)
    jac[...] = jnp.zeros_like(jac)
    acc_cov[...] = jnp.zeros_like(acc_cov)
    acc_jac[...] = jnp.zeros_like(acc_jac)

    coef_copy().wait()
    for p in range(channels):
        coefs[p : p + 1, :] = jnp.full((1, cols), coef_s[p], F32)
    coefs[...] = coefs[...].astype(BF16).astype(F32)

    def residuals(r, carry):
        reg_copy(r).wait()
        at = pl.ds(pl.multiple_of(r * reg_rows, reg_rows), reg_rows)

        def add(q, total):
            for u in range(8):
                p = q * 8 + u
                total = total + reg[p, at, :].astype(F32) * coefs[pl.ds(p, 1), :]
            return total

        fitted = lax.fori_loop(0, channels // 8, add, jnp.zeros((reg_rows, cols), F32))

        @pl.when(r == 0)
        def _():
            outcome_copy().wait()
            land_copy().wait()

        here = land[at, :].astype(F32)
        weighted[at, :] = here * (outcome[at, :] - fitted)
        land_float[at, :] = here
        return carry

    lax.fori_loop(0, 4, residuals, 0)

    def chunk_rows(c):
        return pl.ds(pl.multiple_of(c * CH * SUB, CH * SUB), CH * SUB)

    def to_left(c):
        return pltpu.make_async_remote_copy(
            src_ref=send_l.at[:, chunk_rows(c), :],
            dst_ref=y_r.at[:, chunk_rows(c), :],
            send_sem=yl_send.at[c],
            recv_sem=yr_recv.at[c],
            device_id=(gx, gy - 1),
            device_id_type=MESH,
        )

    def to_right(c):
        return pltpu.make_async_remote_copy(
            src_ref=send_r.at[:, chunk_rows(c), :],
            dst_ref=y_l.at[:, chunk_rows(c), :],
            send_sem=yr_send.at[c],
            recv_sem=yl_recv.at[c],
            device_id=(gx, gy + 1),
            device_id_type=MESH,
        )

    def to_upper(c):
        at = pl.ds(c * CH, CH)
        return pltpu.make_async_remote_copy(
            src_ref=rows_sm.at[:, at, half : 2 * half, :],
            dst_ref=rows_sm.at[:, at, 3 * half : 4 * half, :],
            send_sem=zt_send.at[c],
            recv_sem=zb_recv.at[c],
            device_id=(gx - 1, gy),
            device_id_type=MESH,
        )

    def to_lower(c):
        at = pl.ds(c * CH, CH)
        return pltpu.make_async_remote_copy(
            src_ref=rows_sm.at[:, at, 2 * half : 3 * half, :],
            dst_ref=rows_sm.at[:, at, 0:half, :],
            send_sem=zb_send.at[c],
            recv_sem=zt_recv.at[c],
            device_id=(gx + 1, gy),
            device_id_type=MESH,
        )

    has_left, has_right = gy > 0, gy < ny - 1
    has_upper, has_lower = gx > 0, gx < nx - 1

    first_lanes = iota((2 * SUB, 128), 1) < B

    def store_blocked(ref, first_block, at, one, two):
        ref[first_block, at, :] = jnp.concatenate([one[:SUB], two[:SUB]], axis=0).astype(BF16)
        ref[first_block + 1, at, :] = jnp.concatenate([one[SUB:], two[SUB:]], axis=0).astype(BF16)

    def store_wide(ref, first_block, at, one, two):
        for h in range(2):
            lanes = slice(128 * h, 128 * h + 128)
            store_blocked(ref.at[h], first_block, at, one[:, lanes], two[:, lanes])

    def moments(c, carry):
        inst_copy(c).wait()

        def channel_pair(u, inner):
            k = c * CH + 2 * u
            at = pl.ds(pl.multiple_of(k * SUB, 2 * SUB), 2 * SUB)
            for r in range(0, half, 2 * SUB):
                first = r // SUB
                upper, lower = slice(r, r + 2 * SUB), slice(half + r, half + r + 2 * SUB)
                w_upper, w_lower = weighted[upper, :], weighted[lower, :]
                raw = [(inst[k + v, upper, :].astype(F32), inst[k + v, lower, :].astype(F32)) for v in range(2)]
                prods = [(top * w_upper, bot * w_lower) for top, bot in raw]
                store_wide(inst_b, first, at, raw[0][0], raw[1][0])
                store_wide(inst_b, blocks // 2 + first, at, raw[0][1], raw[1][1])
                store_wide(mom, first, at, prods[0][0], prods[1][0])
                store_wide(mom, blocks // 2 + first, at, prods[0][1], prods[1][1])
                left = [
                    jnp.where(first_lanes, top[:, :128], pltpu.roll(bot[:, :128], B, 1)) for top, bot in prods
                ]
                right = [
                    jnp.where(first_lanes, pltpu.roll(top[:, cols - 128 :], B, 1), bot[:, cols - 128 :])
                    for top, bot in prods
                ]
                store_blocked(send_l, first, at, left[0], left[1])
                store_blocked(send_r, first, at, right[0], right[1])
            return inner

        lax.fori_loop(0, CH // 2, channel_pair, 0)

        @pl.when(c == 0)
        def _():
            pl.semaphore_wait(barrier, nx - 1 + ny - 1)

        @pl.when(has_left)
        def _():
            to_left(c).start()

        @pl.when(has_right)
        def _():
            to_right(c).start()

        return carry

    lax.fori_loop(0, n_chunks, moments, 0)

    def block_regressors(u, carry):
        at = pl.ds(pl.multiple_of(2 * u * SUB, 2 * SUB), 2 * SUB)
        for r in range(0, rows, 2 * SUB):
            here = land_float[r : r + 2 * SUB, :]
            one = reg[2 * u, r : r + 2 * SUB, :].astype(F32) * here
            two = reg[2 * u + 1, r : r + 2 * SUB, :].astype(F32) * here
            store_wide(reg_b, r // SUB, at, one, two)
        return carry

    def product(acc, left_ref, left_rows, right_ref, right_rows, b):
        at = (slice(0, left_rows.size), slice(0, right_rows.size))
        lhs = jnp.concatenate([wide(left_ref, b, left_rows), wide(left_ref, b + 1, left_rows)], axis=1)
        rhs = jnp.concatenate([wide(right_ref, b, right_rows), wide(right_ref, b + 1, right_rows)], axis=1)
        acc[at] += dot_t(lhs, rhs)

    def fold(acc, left_count, right_count, first_column):
        at = (slice(0, left_count * SUB), slice(0, right_count * SUB))
        shape = (1, SUB, right_count * SUB)
        kept = jnp.where(iota(shape, 2) % SUB == iota(shape, 1), acc[at].reshape(left_count, SUB, right_count * SUB), 0.0)
        kept = jnp.sum(kept, axis=1)
        pick = iota((right_count * SUB, 128), 0) // SUB + first_column == iota((right_count * SUB, 128), 1)
        acc[...] = jnp.zeros_like(acc)
        return lax.dot_general(
            kept,
            pick.astype(F32),
            (((1,), (0,)), ((), ())),
            precision=lax.Precision.HIGHEST,
            preferred_element_type=F32,
        )

    def jac_part(first, b):
        at = pl.ds(pl.multiple_of(first * SUB, JAC_BLOCK * SUB), JAC_BLOCK * SUB)
        product(acc_jac, inst_b, pl.ds(0, channels * SUB), reg_b, at, b)

    def jac_fold(first):
        jac[...] += fold(acc_jac, channels, JAC_BLOCK, first)

    def cov_part(first, count, b):
        left = pl.ds(first * SUB, (channels - first) * SUB)
        product(acc_cov, mom, left, sm_b, pl.ds(first * SUB, count * SUB), b)

    def cov_fold(ref, first, count):
        ref[first:, :] += fold(acc_cov, channels - first, count, first)

    def moment_sums(b):
        if b == 0:
            sums[...] = jnp.zeros_like(sums)
        sums[...] += wide(mom, b).astype(F32) + wide(mom, b + 1).astype(F32)

    def smooth_rows(c):
        @pl.when(has_left)
        def _():
            to_right(c).wait_recv()

        @pl.when(has_right)
        def _():
            to_left(c).wait_recv()

        at = chunk_rows(c)
        for start, weights in ((0, w_top), (half, w_bot)):
            lhs = jnp.concatenate(
                [
                    jnp.concatenate([wide(mom, start // SUB + b, at), y_l[b, at, :], y_r[b, at, :]], axis=1)
                    for b in range(half // SUB)
                ],
                axis=0,
            )
            total = dot(lhs, wide(weights)) * (1.0 / (B + 1))
            for b in range(0, half // SUB, 2):
                for u in range(CH):
                    one = total[(b * CH + u) * SUB : (b * CH + u + 1) * SUB]
                    two = total[((b + 1) * CH + u) * SUB : ((b + 1) * CH + u + 1) * SUB]
                    place = half + start + b * SUB
                    both = jnp.concatenate([one, two], axis=0).astype(BF16)
                    rows_sm[0, c * CH + u, place : place + 2 * SUB, :] = both[:, :128]
                    rows_sm[1, c * CH + u, place : place + 2 * SUB, :] = both[:, 128:]

        @pl.when(has_upper)
        def _():
            to_upper(c).start()

        @pl.when(has_lower)
        def _():
            to_lower(c).start()

    def smooth_columns(c):
        @pl.when(has_upper)
        def _():
            to_lower(c).wait_recv()

        @pl.when(has_lower)
        def _():
            to_upper(c).wait_recv()

        for u in range(0, CH, 2):
            k = c * CH + u
            pair = [dot(wide(w_col), wide(rows_sm, k + v)) * (1.0 / (B + 1) ** 2) for v in range(2)]
            sm[k] = pair[0].astype(BF16)
            sm[k + 1] = pair[1].astype(BF16)
            at = pl.ds(pl.multiple_of(k * SUB, 2 * SUB), 2 * SUB)
            for r in range(0, rows, 2 * SUB):
                store_wide(sm_b, r // SUB, at, pair[0][r : r + 2 * SUB], pair[1][r : r + 2 * SUB])

    pieces = channels // 8
    own_pieces = 2 * pieces // nx

    def send_all(number, peers, me, copy):
        def send(o, carry):
            copy(number, (me + o) % peers).start()
            return carry

        lax.fori_loop(1, peers, send, 0)

    def land_all(number, landed):
        pltpu.make_async_copy(landed, landed, ar_recv.at[number]).wait()
        pltpu.make_async_copy(landed, landed, ar_send.at[number]).wait()

    def own(g):
        return pl.ds(g * own_pieces, own_pieces)

    def remote(number, src, dst, device):
        return pltpu.make_async_remote_copy(
            src_ref=src,
            dst_ref=dst,
            send_sem=ar_send.at[number],
            recv_sem=ar_recv.at[number],
            device_id=device,
            device_id_type=MESH,
        )

    def scatter(number, g):
        return remote(number, part.at[own(g)], got1.at[gx], (g, gy))

    def across(number, g):
        return remote(number, sum1, got2.at[gy], (gx, g))

    def gather(number, g):
        return remote(number, sum2, got3.at[own(gx)], (g, gy))

    def tail_x(number, g):
        return remote(number, tile, got4.at[gx], (g, gy))

    def tail_y(number, g):
        return remote(number, sum4, got5.at[gy], (gx, g))

    def early_scatter():
        count = jnp.sum(jnp.sum(land_float[...], axis=0, keepdims=True), axis=1, keepdims=True)
        columns = jnp.sum(jnp.sum(sums[...].reshape(channels, SUB, cols), axis=1), axis=1, keepdims=True)
        right_half = iota((channels, 128), 1) >= channels
        as_row = jnp.sum(
            jnp.where(iota((channels, 128), 1) - channels == iota((channels, 128), 0), columns, 0.0),
            axis=0,
            keepdims=True,
        )
        part[0:pieces] = jnp.where(right_half, count, cov[...]).reshape(pieces, 8, 128)
        part[pieces : 2 * pieces] = jnp.where(right_half, as_row, jac[...]).reshape(pieces, 8, 128)
        got1[gx] = part[own(gx)]
        send_all(0, nx, gx, scatter)

    def early_across():
        land_all(0, got1.at[0 : nx - 1])
        sum1[...] = jnp.sum(got1[...], axis=0)
        got2[gy] = sum1[...]
        send_all(1, ny, gy, across)

    def early_gather():
        land_all(1, got2.at[0 : ny - 1])
        sum2[...] = jnp.sum(got2[...], axis=0)
        got3[own(gx)] = sum2[...]
        send_all(2, nx, gx, gather)

    last = n_chunks + LAG - 1

    def pipeline(t, carry):
        @pl.when(t < n_chunks)
        def _():
            smooth_rows(t)

        @pl.when(t == 0)
        def _():
            lax.fori_loop(0, channels // 2, block_regressors, 0)
            for b in range(0, blocks, 2):
                moment_sums(b)

        for g in range(channels // JAC_BLOCK):

            @pl.when(jnp.logical_or(t == 1 + 2 * g, t == 2 + 2 * g))
            def _(g=g):
                for u in range(0, blocks // 2, 2):
                    jac_part(g * JAC_BLOCK, (t - 1 - 2 * g) * (blocks // 2) + u)

            @pl.when(t == 2 + 2 * g)
            def _(g=g):
                jac_fold(g * JAC_BLOCK)

        first, count = COV_BLOCKS[0]
        begin = (first + count) // CH + LAG

        @pl.when(jnp.logical_or(t == begin, t == begin + 1))
        def _(first=first, count=count, begin=begin):
            for u in range(0, blocks // 2, 2):
                cov_part(first, count, (t - begin) * (blocks // 2) + u)

        @pl.when(t == begin + 1)
        def _(first=first, count=count):
            cov_fold(cov, first, count)
            early_scatter()

        first, count = COV_BLOCKS[1]
        begin = (first + count) // CH + LAG

        @pl.when(t == begin)
        def _(first=first, count=count):
            early_across()
            for b in range(0, blocks, 2):
                cov_part(first, count, b)
            cov_fold(cov_tail, first, count)

        @pl.when(t == last)
        def _():
            early_gather()

        @pl.when(t >= LAG)
        def _():
            smooth_columns(t - LAG)

        return carry

    lax.fori_loop(0, last + 1, pipeline, 0)

    first, count = COV_BLOCKS[2]
    for b in range(0, blocks, 2):
        cov_part(first, count, b)
    cov_fold(cov_tail, first, count)

    lane_group = iota((8, 128), 1) // 32
    packed = jnp.zeros((8, 128), F32)
    for g in range((channels - TAIL) // 8):
        piece = cov_tail[TAIL + 8 * g : TAIL + 8 * g + 8, :]
        packed = jnp.where(lane_group == g, pltpu.roll(piece, (32 * g - TAIL) % 128, 1), packed)
    tile[...] = packed
    send_all(3, nx, gx, tail_x)
    got4[gx] = tile[...]

    def drain(c, carry):
        @pl.when(has_left)
        def _():
            to_left(c).wait_send()

        @pl.when(has_right)
        def _():
            to_right(c).wait_send()

        @pl.when(has_upper)
        def _():
            to_upper(c).wait_send()

        @pl.when(has_lower)
        def _():
            to_lower(c).wait_send()

        return carry

    lax.fori_loop(0, n_chunks, drain, 0)
    land_all(2, got3.at[0 : (nx - 1) * own_pieces])
    total_v[...] = got3[...].reshape(2 * channels, 128)

    land_all(3, got4.at[0 : nx - 1])
    sum4[...] = jnp.sum(got4[...], axis=0)
    send_all(4, ny, gy, tail_y)
    got5[gy] = sum4[...]
    land_all(4, got5.at[0 : ny - 1])
    tail_v[...] = jnp.sum(got5[...], axis=0)


def finish(s_in, total_v, tail_v, coef_v, wgt_v, s_out, hac_v, new_v, sem):
    channels = s_in.shape[0]
    share = channels // 16

    def move(c):
        at = pl.ds(c * share, share)
        return pltpu.make_async_copy(s_in.at[at], s_out.at[at], sem.at[c])

    for c in range(16):
        move(c).start()
    first, second = total_v[0:channels, :], total_v[channels : 2 * channels, :]
    land_total = first[:, channels : channels + 1]
    tail = jnp.concatenate([pltpu.roll(tail_v[...], (TAIL - 32 * g) % 128, 1) for g in range((channels - TAIL) // 8)], axis=0)
    bottom = jnp.where(iota(tail.shape, 1) >= TAIL, tail, first[TAIL:, :])
    lower = jnp.concatenate([first[:TAIL, :], bottom], axis=0)[:, :channels]
    row, column = iota((channels, channels), 0), iota((channels, channels), 1)
    held = row >= 0
    for start, count in COV_BLOCKS:
        held = jnp.logical_and(held, jnp.logical_or(column < start, row >= start))
    hac_v[...] = jnp.where(held, lower, lower.T) * ((B + 1) / land_total)
    mean = second[0:1, channels:] / land_total[0:1, :]
    weighed = jnp.sum(wgt_v[...] * mean, axis=1, keepdims=True)
    jacobian = -second[:, :channels] / land_total
    gradient = 2.0 * jnp.sum(jacobian * weighed, axis=0, keepdims=True)
    new_v[...] = coef_v[...] - step_rate * gradient
    for c in range(16):
        move(c).wait()


def local(nx, ny, instruments, regressors, outcome, land_mask, coefficients, weighting):
    channels, rows, cols = instruments.shape
    n_chunks = channels // CH
    pieces = channels // 8
    own = 2 * pieces // nx
    blocks = rows // SUB
    any_spec = pl.BlockSpec(memory_space=pl.ANY)
    in_hbm = functools.partial(pltpu.with_memory_space_constraint, memory_space=pltpu.HBM)
    in_vmem = functools.partial(pltpu.with_memory_space_constraint, memory_space=pltpu.VMEM)
    hbm_spec = pl.BlockSpec(memory_space=pltpu.HBM)
    vmem_spec = pl.BlockSpec(memory_space=pltpu.VMEM)
    dma = pltpu.SemaphoreType.DMA
    blocked = pltpu.VMEM((2, blocks, channels * SUB, 128), BF16)
    edge = pltpu.VMEM((blocks // 2, channels * SUB, 128), BF16)
    smoothed, totals, tail = pl.pallas_call(
        functools.partial(kernel, nx, ny),
        out_shape=(
            pltpu.VMEM((channels, rows, cols), BF16),
            pltpu.VMEM((2 * channels, 128), F32),
            pltpu.VMEM((8, 128), F32),
        ),
        in_specs=[hbm_spec] * 5,
        out_specs=(vmem_spec, vmem_spec, vmem_spec),
        scratch_shapes=[
            pltpu.VMEM((channels, rows, cols), BF16),
            pltpu.VMEM((channels, rows, cols), BF16),
            pltpu.VMEM((rows, cols), F32),
            pltpu.VMEM((rows, cols), jnp.int32),
            pltpu.SMEM((channels,), F32),
            pltpu.VMEM((channels, cols), F32),
            pltpu.VMEM((rows, cols), F32),
            pltpu.VMEM((rows, cols), F32),
            blocked,
            blocked,
            blocked,
            edge,
            edge,
            edge,
            edge,
            pltpu.VMEM((2, channels, 2 * rows, 128), BF16),
            blocked,
            pltpu.VMEM((2, 2 * cols, 128), BF16),
            pltpu.VMEM((2, 2 * cols, 128), BF16),
            pltpu.VMEM((2, rows, 128), BF16),
            pltpu.VMEM((channels * SUB, 32 * SUB), F32),
            pltpu.VMEM((channels * SUB, 32 * SUB), F32),
            pltpu.VMEM((channels, 128), F32),
            pltpu.VMEM((channels, 128), F32),
            pltpu.VMEM((channels, 128), F32),
            pltpu.VMEM((channels * SUB, cols), F32),
            pltpu.VMEM((2 * pieces, 8, 128), F32),
            pltpu.VMEM((nx, own, 8, 128), F32),
            pltpu.VMEM((own, 8, 128), F32),
            pltpu.VMEM((ny, own, 8, 128), F32),
            pltpu.VMEM((own, 8, 128), F32),
            pltpu.VMEM((2 * pieces, 8, 128), F32),
            pltpu.VMEM((8, 128), F32),
            pltpu.VMEM((nx, 8, 128), F32),
            pltpu.VMEM((8, 128), F32),
            pltpu.VMEM((ny, 8, 128), F32),
            dma((3,)),
            dma((4,)),
            dma((n_chunks,)),
        ]
        + [dma((n_chunks,))] * 8
        + [dma((5,)), dma((5,))],
        compiler_params=pltpu.CompilerParams(
            collective_id=0, has_side_effects=True, vmem_limit_bytes=42 * 1024 * 1024
        ),
        cost_estimate=pl.CostEstimate(flops=5 * 10**9, bytes_accessed=13 * 2**20, transcendentals=0),
    )(*map(in_hbm, (instruments, regressors, outcome, land_mask, coefficients)))
    smoothed, hac_cov, new_coefficients = pl.pallas_call(
        finish,
        out_shape=(
            jax.ShapeDtypeStruct((channels, rows, cols), BF16),
            jax.ShapeDtypeStruct((channels, channels), F32),
            jax.ShapeDtypeStruct((1, channels), F32),
        ),
        in_specs=[vmem_spec] * 5,
        out_specs=(any_spec, vmem_spec, vmem_spec),
        scratch_shapes=[dma((16,))],
        compiler_params=pltpu.CompilerParams(vmem_limit_bytes=4 * 1024 * 1024),
        cost_estimate=pl.CostEstimate(flops=10**6, bytes_accessed=8 * 2**20, transcendentals=0),
    )(in_vmem(smoothed), in_vmem(totals), in_vmem(tail), coefficients.reshape(1, channels), weighting)
    return smoothed, hac_cov, new_coefficients.reshape(channels)


def solution(mesh):
    placed = (P(None, "gx", "gy"), P(None, "gx", "gy"), P("gx", "gy"), P("gx", "gy"), P(), P())
    return jax.shard_map(
        functools.partial(local, mesh.shape["gx"], mesh.shape["gy"]),
        mesh=mesh,
        in_specs=placed,
        out_specs=(P(None, "gx", "gy"), P(), P()),
        check_vma=False,
    )
```

time: 88.9 us -> 63.6 us (0.72)
  Pallas kernels: 81.7 us -> 62.8 us
  local copies, waits for them, and re-layouts: 6.35 us -> 0.01 us
    pallas_call x1 -> x2, Pallas kernels: 81.7 us -> 62.8 us  [the longest x1 60 us: local(): pl.pallas_call(functools.partial(kernel, nx, ny), out_shape=(pltpu.VMEM((...]
    unnamed x11 -> x4, local copies, waits for them, and re-layouts: 6.35 us -> 0.01 us
where the time goes in v2:
time: 63.6 us; the launch traced here: 63.5 us
  Pallas kernels  62.8 us (99%)
  between operations  0.67 us (1%)
    pallas_call x1, Pallas kernels, local(): pl.pallas_call(functools.partial(kernel, nx, ny), out_shape=(pltpu.VMEM((...  60 us
    pallas_call x1, Pallas kernels, local(): pl.pallas_call(finish, out_shape=(jax.ShapeDtypeStruct((channels, rows, c...  2.75 us

profile of v2, /device:TPU:1, one launch (start us, length us, event | category | flops | bytes accessed | tf_op | source)
XLA Modules:
  0.0 63.5 jit_solution(3732879713309056707)
XLA Ops:
  0.6 0.0 copy-start
  0.6 0.0 copy-start.1
  0.7 60.0 %shard_map.85 = (bf16[64,128,256]{2,1,0:T(8,128)(2,1)S(1)}, f32[128,128]{1,0:T(8,128)S(1)}, f32[8,128]{1,0:T(8,128)S(1)}) custom-call(bf16[64,128,256]{2,1,0:T(8,128)(2,1)} %inst_h.1, bf16[64,128,256]{2,1,0:T(8,128)(2,1)} %reg_h.1, f32[128,256]{1,0:T(8,128)} %outcome_h.1, s32[128,256]{1,0:T(8,128)} %land_h.1, f32[64]{0:T(128)} %coef_h.1), custom_call_target="tpu_custom_call" | custom-call | flops 5000000000 | bytes 13631488 | tf_op jit(solution)/shard_map/pallas_call | solution.py:647
  60.7 0.0 copy-done
  60.7 0.0 copy-done.1
  60.7 2.8 %shard_map.86 = (bf16[64,128,256]{2,1,0:T(8,128)(2,1)}, f32[64,64]{1,0:T(8,128)}, f32[1,64]{1,0:T(1,128)}) custom-call(bf16[64,128,256]{2,1,0:T(8,128)(2,1)S(1)} %get-tuple-element.9.s_in, f32[128,128]{1,0:T(8,128)S(1)} %get-tuple-element.10.total_v, f32[8,128]{1,0:T(8,128)S(1)} %get-tuple-element.11.tail_v, f32[1,64]{1,0:T(1,128)S(1)} %bitcast.2, ...), custom_call_target="tpu_custom_call" | custom-call | flops 1000000 | bytes 8388608 | tf_op jit(solution)/shard_map/pallas_call | solution.py:704
Async XLA Ops:
  0.6 60.1 %copy-start = (f32[64,64]{1,0:T(8,128)S(1)}, f32[64,64]{1,0:T(8,128)}, u32[]{:S(2)}) copy-start(f32[64,64]{1,0:T(8,128)} %wgt_v.1) | copy-start | bytes 49156
  0.6 60.1 %copy-start.1 = (f32[64]{0:T(128)S(1)}, f32[64]{0:T(128)}, u32[]{:S(2)}) copy-start(f32[64]{0:T(128)} %coef_h.1) | copy-start | bytes 772

commit v3 on v2

--- a/solution.py
+++ b/solution.py
@@ -14,6 +14,7 @@
 BF16 = jnp.bfloat16
 CH = 8
 SUB = 8
+AHEAD = 2
 LAG = 1
 COV_BLOCKS = ((0, 32), (32, 16), (48, 16))
 JAC_BLOCK = 32
@@ -195,7 +196,7 @@
 
     coef_copy().wait()
     for p in range(channels):
-        coefs[p : p + 1, :] = jnp.full((1, cols), coef_s[p], F32)
+        coefs[p] = jnp.full((SUB, 128), coef_s[p], F32)
     coefs[...] = coefs[...].astype(BF16).astype(F32)
 
     def residuals(r, carry):
@@ -205,7 +206,8 @@
         def add(q, total):
             for u in range(8):
                 p = q * 8 + u
-                total = total + reg[p, at, :].astype(F32) * coefs[pl.ds(p, 1), :]
+                one = jnp.concatenate([coefs[p]] * (cols // 128), axis=1)
+                total = total + reg[p, at, :].astype(F32) * jnp.concatenate([one] * (reg_rows // SUB), axis=0)
             return total
 
         fitted = lax.fori_loop(0, channels // 8, add, jnp.zeros((reg_rows, cols), F32))
@@ -269,6 +271,15 @@
 
     has_left, has_right = gy > 0, gy < ny - 1
     has_upper, has_lower = gx > 0, gx < nx - 1
+
+    def send_edges(c):
+        @pl.when(has_left)
+        def _():
+            to_left(c).start()
+
+        @pl.when(has_right)
+        def _():
+            to_right(c).start()
 
     first_lanes = iota((2 * SUB, 128), 1) < B
 
@@ -314,13 +325,9 @@
         def _():
             pl.semaphore_wait(barrier, nx - 1 + ny - 1)
 
-        @pl.when(has_left)
-        def _():
-            to_left(c).start()
-
-        @pl.when(has_right)
-        def _():
-            to_right(c).start()
+        @pl.when(c < AHEAD)
+        def _():
+            send_edges(c)
 
         return carry
 
@@ -504,6 +511,10 @@
         def _():
             smooth_rows(t)
 
+        @pl.when(t + AHEAD < n_chunks)
+        def _():
+            send_edges(t + AHEAD)
+
         @pl.when(t == 0)
         def _():
             lax.fori_loop(0, channels // 2, block_regressors, 0)
@@ -603,13 +614,13 @@
 
 def finish(s_in, total_v, tail_v, coef_v, wgt_v, s_out, hac_v, new_v, sem):
     channels = s_in.shape[0]
-    share = channels // 16
+    share = channels // 4
 
     def move(c):
         at = pl.ds(c * share, share)
         return pltpu.make_async_copy(s_in.at[at], s_out.at[at], sem.at[c])
 
-    for c in range(16):
+    for c in range(4):
         move(c).start()
     first, second = total_v[0:channels, :], total_v[channels : 2 * channels, :]
     land_total = first[:, channels : channels + 1]
@@ -626,7 +637,7 @@
     jacobian = -second[:, :channels] / land_total
     gradient = 2.0 * jnp.sum(jacobian * weighed, axis=0, keepdims=True)
     new_v[...] = coef_v[...] - step_rate * gradient
-    for c in range(16):
+    for c in range(4):
         move(c).wait()
 
 
@@ -659,7 +670,7 @@
             pltpu.VMEM((rows, cols), F32),
             pltpu.VMEM((rows, cols), jnp.int32),
             pltpu.SMEM((channels,), F32),
-            pltpu.VMEM((channels, cols), F32),
+            pltpu.VMEM((channels, SUB, 128), F32),
             pltpu.VMEM((rows, cols), F32),
             pltpu.VMEM((rows, cols), F32),
             blocked,
@@ -710,7 +721,7 @@
         ),
         in_specs=[vmem_spec] * 5,
         out_specs=(any_spec, vmem_spec, vmem_spec),
-        scratch_shapes=[dma((16,))],
+        scratch_shapes=[dma((4,))],
         compiler_params=pltpu.CompilerParams(vmem_limit_bytes=4 * 1024 * 1024),
         cost_estimate=pl.CostEstimate(flops=10**6, bytes_accessed=8 * 2**20, transcendentals=0),
     )(in_vmem(smoothed), in_vmem(totals), in_vmem(tail), coefficients.reshape(1, channels), weighting)

time: 63.6 us -> 63.9 us (level)
  no operation moved by 1% of the time
where the time goes in v3:
time: 63.9 us; the launch traced here: 63.8 us
  Pallas kernels  63.1 us (99%)
  between operations  0.67 us (1%)
    pallas_call x1, Pallas kernels, local(): pl.pallas_call(functools.partial(kernel, nx, ny), out_shape=(pltpu.VMEM((...  60.5 us
    pallas_call x1, Pallas kernels, local(): pl.pallas_call(finish, out_shape=(jax.ShapeDtypeStruct((channels, rows, c...  2.66 us

profile of v3, /device:TPU:1, one launch (start us, length us, event | category | flops | bytes accessed | tf_op | source)
XLA Modules:
  0.0 63.8 jit_solution(6206233924131003182)
XLA Ops:
  0.6 0.0 copy-start
  0.6 0.0 copy-start.1
  0.7 60.5 %shard_map.85 = (bf16[64,128,256]{2,1,0:T(8,128)(2,1)S(1)}, f32[128,128]{1,0:T(8,128)S(1)}, f32[8,128]{1,0:T(8,128)S(1)}) custom-call(bf16[64,128,256]{2,1,0:T(8,128)(2,1)} %inst_h.1, bf16[64,128,256]{2,1,0:T(8,128)(2,1)} %reg_h.1, f32[128,256]{1,0:T(8,128)} %outcome_h.1, s32[128,256]{1,0:T(8,128)} %land_h.1, f32[64]{0:T(128)} %coef_h.1), custom_call_target="tpu_custom_call" | custom-call | flops 5000000000 | bytes 13631488 | tf_op jit(solution)/shard_map/pallas_call | solution.py:658
  61.1 0.0 copy-done
  61.1 0.0 copy-done.1
  61.1 2.7 %shard_map.86 = (bf16[64,128,256]{2,1,0:T(8,128)(2,1)}, f32[64,64]{1,0:T(8,128)}, f32[1,64]{1,0:T(1,128)}) custom-call(bf16[64,128,256]{2,1,0:T(8,128)(2,1)S(1)} %get-tuple-element.9.s_in, f32[128,128]{1,0:T(8,128)S(1)} %get-tuple-element.10.total_v, f32[8,128]{1,0:T(8,128)S(1)} %get-tuple-element.11.tail_v, f32[1,64]{1,0:T(1,128)S(1)} %bitcast.2, ...), custom_call_target="tpu_custom_call" | custom-call | flops 1000000 | bytes 8388608 | tf_op jit(solution)/shard_map/pallas_call | solution.py:715
Async XLA Ops:
  0.6 60.5 %copy-start = (f32[64,64]{1,0:T(8,128)S(1)}, f32[64,64]{1,0:T(8,128)}, u32[]{:S(2)}) copy-start(f32[64,64]{1,0:T(8,128)} %wgt_v.1) | copy-start | bytes 49156
  0.6 60.5 %copy-start.1 = (f32[64]{0:T(128)S(1)}, f32[64]{0:T(128)}, u32[]{:S(2)}) copy-start(f32[64]{0:T(128)} %coef_h.1) | copy-start | bytes 772

commit v4 on v3

--- a/solution.py
+++ b/solution.py
@@ -14,7 +14,7 @@
 BF16 = jnp.bfloat16
 CH = 8
 SUB = 8
-AHEAD = 2
+DEEP = 4
 LAG = 1
 COV_BLOCKS = ((0, 32), (32, 16), (48, 16))
 JAC_BLOCK = 32
@@ -325,10 +325,7 @@
         def _():
             pl.semaphore_wait(barrier, nx - 1 + ny - 1)
 
-        @pl.when(c < AHEAD)
-        def _():
-            send_edges(c)
-
+        send_edges(c)
         return carry
 
     lax.fori_loop(0, n_chunks, moments, 0)
@@ -344,8 +341,8 @@
 
     def product(acc, left_ref, left_rows, right_ref, right_rows, b):
         at = (slice(0, left_rows.size), slice(0, right_rows.size))
-        lhs = jnp.concatenate([wide(left_ref, b, left_rows), wide(left_ref, b + 1, left_rows)], axis=1)
-        rhs = jnp.concatenate([wide(right_ref, b, right_rows), wide(right_ref, b + 1, right_rows)], axis=1)
+        lhs = jnp.concatenate([wide(left_ref, b + u, left_rows) for u in range(DEEP)], axis=1)
+        rhs = jnp.concatenate([wide(right_ref, b + u, right_rows) for u in range(DEEP)], axis=1)
         acc[at] += dot_t(lhs, rhs)
 
     def fold(acc, left_count, right_count, first_column):
@@ -418,15 +415,16 @@
         def _():
             to_lower(c).start()
 
+    def land_columns(c):
+        @pl.when(has_upper)
+        def _():
+            to_lower(c).wait_recv()
+
+        @pl.when(has_lower)
+        def _():
+            to_upper(c).wait_recv()
+
     def smooth_columns(c):
-        @pl.when(has_upper)
-        def _():
-            to_lower(c).wait_recv()
-
-        @pl.when(has_lower)
-        def _():
-            to_upper(c).wait_recv()
-
         for u in range(0, CH, 2):
             k = c * CH + u
             pair = [dot(wide(w_col), wide(rows_sm, k + v)) * (1.0 / (B + 1) ** 2) for v in range(2)]
@@ -511,22 +509,23 @@
         def _():
             smooth_rows(t)
 
-        @pl.when(t + AHEAD < n_chunks)
-        def _():
-            send_edges(t + AHEAD)
-
         @pl.when(t == 0)
         def _():
             lax.fori_loop(0, channels // 2, block_regressors, 0)
             for b in range(0, blocks, 2):
                 moment_sums(b)
 
+        @pl.when(t >= LAG)
+        def _():
+            land_columns(t - LAG)
+
+        @pl.when(jnp.logical_and(t >= 1, t <= 4))
+        def _():
+            for u in range(0, blocks // 2, DEEP):
+                jac_part((t - 1) // 2 * JAC_BLOCK, (t - 1) % 2 * (blocks // 2) + u)
+            smooth_columns(t - LAG)
+
         for g in range(channels // JAC_BLOCK):
-
-            @pl.when(jnp.logical_or(t == 1 + 2 * g, t == 2 + 2 * g))
-            def _(g=g):
-                for u in range(0, blocks // 2, 2):
-                    jac_part(g * JAC_BLOCK, (t - 1 - 2 * g) * (blocks // 2) + u)
 
             @pl.when(t == 2 + 2 * g)
             def _(g=g):
@@ -537,8 +536,9 @@
 
         @pl.when(jnp.logical_or(t == begin, t == begin + 1))
         def _(first=first, count=count, begin=begin):
-            for u in range(0, blocks // 2, 2):
+            for u in range(0, blocks // 2, DEEP):
                 cov_part(first, count, (t - begin) * (blocks // 2) + u)
+            smooth_columns(t - LAG)
 
         @pl.when(t == begin + 1)
         def _(first=first, count=count):
@@ -551,16 +551,14 @@
         @pl.when(t == begin)
         def _(first=first, count=count):
             early_across()
-            for b in range(0, blocks, 2):
+            for b in range(0, blocks, DEEP):
                 cov_part(first, count, b)
+            smooth_columns(t - LAG)
             cov_fold(cov_tail, first, count)
 
         @pl.when(t == last)
         def _():
             early_gather()
-
-        @pl.when(t >= LAG)
-        def _():
             smooth_columns(t - LAG)
 
         return carry
@@ -568,7 +566,7 @@
     lax.fori_loop(0, last + 1, pipeline, 0)
 
     first, count = COV_BLOCKS[2]
-    for b in range(0, blocks, 2):
+    for b in range(0, blocks, DEEP):
         cov_part(first, count, b)
     cov_fold(cov_tail, first, count)
 

time: 63.9 us -> 65.5 us (1.025)
  Pallas kernels: 63.1 us -> 64.8 us
    pallas_call x1, Pallas kernels: 60.5 us -> 62.1 us  [local(): pl.pallas_call(functools.partial(kernel, nx, ny), out_shape=(pltpu.VMEM((...]
where the time goes in v4:
time: 65.5 us
  Pallas kernels  64.8 us (99%)
  between operations  0.67 us (1%)
    pallas_call x1, Pallas kernels, local(): pl.pallas_call(functools.partial(kernel, nx, ny), out_shape=(pltpu.VMEM((...  62.1 us
    pallas_call x1, Pallas kernels, local(): pl.pallas_call(finish, out_shape=(jax.ShapeDtypeStruct((channels, rows, c...  2.66 us

profile of v4, /device:TPU:1, one launch (start us, length us, event | category | flops | bytes accessed | tf_op | source)
XLA Modules:
  0.0 65.5 jit_solution(6345960206763474574)
XLA Ops:
  0.6 0.0 copy-start
  0.6 0.0 copy-start.1
  0.7 62.1 %shard_map.85 = (bf16[64,128,256]{2,1,0:T(8,128)(2,1)S(1)}, f32[128,128]{1,0:T(8,128)S(1)}, f32[8,128]{1,0:T(8,128)S(1)}) custom-call(bf16[64,128,256]{2,1,0:T(8,128)(2,1)} %inst_h.1, bf16[64,128,256]{2,1,0:T(8,128)(2,1)} %reg_h.1, f32[128,256]{1,0:T(8,128)} %outcome_h.1, s32[128,256]{1,0:T(8,128)} %land_h.1, f32[64]{0:T(128)} %coef_h.1), custom_call_target="tpu_custom_call" | custom-call | flops 5000000000 | bytes 13631488 | tf_op jit(solution)/shard_map/pallas_call | solution.py:656
  62.8 0.0 copy-done
  62.8 0.0 copy-done.1
  62.8 2.7 %shard_map.86 = (bf16[64,128,256]{2,1,0:T(8,128)(2,1)}, f32[64,64]{1,0:T(8,128)}, f32[1,64]{1,0:T(1,128)}) custom-call(bf16[64,128,256]{2,1,0:T(8,128)(2,1)S(1)} %get-tuple-element.9.s_in, f32[128,128]{1,0:T(8,128)S(1)} %get-tuple-element.10.total_v, f32[8,128]{1,0:T(8,128)S(1)} %get-tuple-element.11.tail_v, f32[1,64]{1,0:T(1,128)S(1)} %bitcast.2, ...), custom_call_target="tpu_custom_call" | custom-call | flops 1000000 | bytes 8388608 | tf_op jit(solution)/shard_map/pallas_call | solution.py:713
Async XLA Ops:
  0.6 62.1 %copy-start = (f32[64,64]{1,0:T(8,128)S(1)}, f32[64,64]{1,0:T(8,128)}, u32[]{:S(2)}) copy-start(f32[64,64]{1,0:T(8,128)} %wgt_v.1) | copy-start | bytes 49156
  0.6 62.1 %copy-start.1 = (f32[64]{0:T(128)S(1)}, f32[64]{0:T(128)}, u32[]{:S(2)}) copy-start(f32[64]{0:T(128)} %coef_h.1) | copy-start | bytes 772

commit v5 on v3

--- a/solution.py
+++ b/solution.py
@@ -14,7 +14,6 @@
 BF16 = jnp.bfloat16
 CH = 8
 SUB = 8
-AHEAD = 2
 LAG = 1
 COV_BLOCKS = ((0, 32), (32, 16), (48, 16))
 JAC_BLOCK = 32
@@ -74,9 +73,10 @@
     y_r,
     rows_sm,
     sm_b,
-    w_top,
-    w_bot,
+    w_own,
+    w_edge,
     w_col,
+    edges,
     acc_cov,
     acc_jac,
     cov,
@@ -156,13 +156,13 @@
 
     src = iota((cols, cols), 0)
     dst = iota((cols, cols), 1)
-    own_band = hat(src - dst)
-    low = src % half
-    side = jnp.where(src < 2 * half, low - half, low + cols)
-    ramp = jnp.maximum(B + 1 - jnp.abs(side - dst), 0).astype(F32)
-    is_top = (src // half) % 2 == 0
-    put_wide(w_top, jnp.concatenate([own_band, jnp.where(is_top, ramp, 0.0).astype(BF16)], axis=0))
-    put_wide(w_bot, jnp.concatenate([own_band, jnp.where(is_top, 0.0, ramp).astype(BF16)], axis=0))
+    put_wide(w_own, hat(src - dst))
+    lane = jnp.bitwise_and(dst, 127)
+    column = jnp.where(lane < B, lane, lane + cols - 128)
+    low = jnp.bitwise_and(src, B - 1)
+    side = jnp.where(src < 2 * B, low - B, low + cols)
+    same_half = (jnp.bitwise_and(src, B) == 0) == (dst < 128)
+    put_wide(w_edge, jnp.where(same_half, jnp.maximum(B + 1 - jnp.abs(side - column), 0), 0).astype(F32).astype(BF16))
     put_wide(w_col, hat(iota((rows, 2 * rows), 1) - half - iota((rows, 2 * rows), 0)))
 
     @pl.when(gy == 0)
@@ -325,10 +325,7 @@
         def _():
             pl.semaphore_wait(barrier, nx - 1 + ny - 1)
 
-        @pl.when(c < AHEAD)
-        def _():
-            send_edges(c)
-
+        send_edges(c)
         return carry
 
     lax.fori_loop(0, n_chunks, moments, 0)
@@ -344,16 +341,16 @@
 
     def product(acc, left_ref, left_rows, right_ref, right_rows, b):
         at = (slice(0, left_rows.size), slice(0, right_rows.size))
-        lhs = jnp.concatenate([wide(left_ref, b, left_rows), wide(left_ref, b + 1, left_rows)], axis=1)
-        rhs = jnp.concatenate([wide(right_ref, b, right_rows), wide(right_ref, b + 1, right_rows)], axis=1)
-        acc[at] += dot_t(lhs, rhs)
+        for u in range(2):
+            acc[at] += dot_t(wide(left_ref, b + u, left_rows), wide(right_ref, b + u, right_rows))
 
     def fold(acc, left_count, right_count, first_column):
         at = (slice(0, left_count * SUB), slice(0, right_count * SUB))
         shape = (1, SUB, right_count * SUB)
-        kept = jnp.where(iota(shape, 2) % SUB == iota(shape, 1), acc[at].reshape(left_count, SUB, right_count * SUB), 0.0)
+        kept = jnp.where(jnp.bitwise_and(iota(shape, 2), SUB - 1) == iota(shape, 1), acc[at].reshape(left_count, SUB, right_count * SUB), 0.0)
         kept = jnp.sum(kept, axis=1)
-        pick = iota((right_count * SUB, 128), 0) // SUB + first_column == iota((right_count * SUB, 128), 1)
+        from_pick = iota((right_count * SUB, 128), 0) - (iota((right_count * SUB, 128), 1) - first_column) * SUB
+        pick = jnp.logical_and(from_pick >= 0, from_pick < SUB)
         acc[...] = jnp.zeros_like(acc)
         return lax.dot_general(
             kept,
@@ -377,10 +374,13 @@
     def cov_fold(ref, first, count):
         ref[first:, :] += fold(acc_cov, channels - first, count, first)
 
-    def moment_sums(b):
-        if b == 0:
-            sums[...] = jnp.zeros_like(sums)
-        sums[...] += wide(mom, b).astype(F32) + wide(mom, b + 1).astype(F32)
+    def moment_sums(q, carry):
+        at = pl.ds(pl.multiple_of(q * 64, 64), 64)
+        total = wide(mom, 0, at).astype(F32)
+        for b in range(1, blocks):
+            total = total + wide(mom, b, at).astype(F32)
+        sums[at, :] = total
+        return carry
 
     def smooth_rows(c):
         @pl.when(has_left)
@@ -392,23 +392,28 @@
             to_left(c).wait_recv()
 
         at = chunk_rows(c)
-        for start, weights in ((0, w_top), (half, w_bot)):
-            lhs = jnp.concatenate(
-                [
-                    jnp.concatenate([wide(mom, start // SUB + b, at), y_l[b, at, :], y_r[b, at, :]], axis=1)
-                    for b in range(half // SUB)
-                ],
-                axis=0,
-            )
-            total = dot(lhs, wide(weights)) * (1.0 / (B + 1))
-            for b in range(0, half // SUB, 2):
+        n_half = half // SUB
+        outer = jnp.concatenate(
+            [jnp.concatenate([y_l[b, at, :], y_r[b, at, :]], axis=1) for b in range(n_half)], axis=0
+        )
+        edges[...] = dot(outer, wide(w_edge))
+        first_64 = iota((SUB, 128), 1) < B
+        for h in range(2):
+            lhs = jnp.concatenate([wide(mom, h * n_half + b, at) for b in range(n_half)], axis=0)
+            total = dot(lhs, wide(w_own))
+            edges_here = edges[:, 128 * h : 128 * h + 128]
+            for b in range(0, n_half, 2):
                 for u in range(CH):
-                    one = total[(b * CH + u) * SUB : (b * CH + u + 1) * SUB]
-                    two = total[((b + 1) * CH + u) * SUB : ((b + 1) * CH + u + 1) * SUB]
-                    place = half + start + b * SUB
-                    both = jnp.concatenate([one, two], axis=0).astype(BF16)
-                    rows_sm[0, c * CH + u, place : place + 2 * SUB, :] = both[:, :128]
-                    rows_sm[1, c * CH + u, place : place + 2 * SUB, :] = both[:, 128:]
+                    place = half + h * half + b * SUB
+                    tiles = ([], [])
+                    for v in range(2):
+                        piece = slice(((b + v) * CH + u) * SUB, ((b + v) * CH + u + 1) * SUB)
+                        edge = edges_here[piece]
+                        tiles[0].append(total[piece, :128] + jnp.where(first_64, edge, 0.0))
+                        tiles[1].append(total[piece, 128:] + jnp.where(first_64, 0.0, edge))
+                    for w in range(2):
+                        both = jnp.concatenate(tiles[w], axis=0) * (1.0 / (B + 1))
+                        rows_sm[w, c * CH + u, place : place + 2 * SUB, :] = both.astype(BF16)
 
         @pl.when(has_upper)
         def _():
@@ -511,15 +516,10 @@
         def _():
             smooth_rows(t)
 
-        @pl.when(t + AHEAD < n_chunks)
-        def _():
-            send_edges(t + AHEAD)
-
         @pl.when(t == 0)
         def _():
             lax.fori_loop(0, channels // 2, block_regressors, 0)
-            for b in range(0, blocks, 2):
-                moment_sums(b)
+            lax.fori_loop(0, channels * SUB // 64, moment_sums, 0)
 
         for g in range(channels // JAC_BLOCK):
 
@@ -682,9 +682,10 @@
             edge,
             pltpu.VMEM((2, channels, 2 * rows, 128), BF16),
             blocked,
-            pltpu.VMEM((2, 2 * cols, 128), BF16),
-            pltpu.VMEM((2, 2 * cols, 128), BF16),
+            pltpu.VMEM((2, cols, 128), BF16),
+            pltpu.VMEM((2, cols, 128), BF16),
             pltpu.VMEM((2, rows, 128), BF16),
+            pltpu.VMEM((blocks // 2 * CH * SUB, cols), F32),
             pltpu.VMEM((channels * SUB, 32 * SUB), F32),
             pltpu.VMEM((channels * SUB, 32 * SUB), F32),
             pltpu.VMEM((channels, 128), F32),

time: 63.9 us -> 63.3 us (level)
  no operation moved by 1% of the time
where the time goes in v5:
time: 63.3 us; the launch traced here: 63.2 us
  Pallas kernels  62.5 us (99%)
  between operations  0.67 us (1%)
    pallas_call x1, Pallas kernels, local(): pl.pallas_call(functools.partial(kernel, nx, ny), out_shape=(pltpu.VMEM((...  59.8 us
    pallas_call x1, Pallas kernels, local(): pl.pallas_call(finish, out_shape=(jax.ShapeDtypeStruct((channels, rows, c...  2.66 us

profile of v5, /device:TPU:1, one launch (start us, length us, event | category | flops | bytes accessed | tf_op | source)
XLA Modules:
  0.0 63.2 jit_solution(15831576491376418772)
XLA Ops:
  0.6 0.0 copy-start
  0.6 0.0 copy-start.1
  0.7 59.8 %shard_map.85 = (bf16[64,128,256]{2,1,0:T(8,128)(2,1)S(1)}, f32[128,128]{1,0:T(8,128)S(1)}, f32[8,128]{1,0:T(8,128)S(1)}) custom-call(bf16[64,128,256]{2,1,0:T(8,128)(2,1)} %inst_h.1, bf16[64,128,256]{2,1,0:T(8,128)(2,1)} %reg_h.1, f32[128,256]{1,0:T(8,128)} %outcome_h.1, s32[128,256]{1,0:T(8,128)} %land_h.1, f32[64]{0:T(128)} %coef_h.1), custom_call_target="tpu_custom_call" | custom-call | flops 5000000000 | bytes 13631488 | tf_op jit(solution)/shard_map/pallas_call | solution.py:658
  60.5 0.0 copy-done
  60.5 0.0 copy-done.1
  60.5 2.7 %shard_map.86 = (bf16[64,128,256]{2,1,0:T(8,128)(2,1)}, f32[64,64]{1,0:T(8,128)}, f32[1,64]{1,0:T(1,128)}) custom-call(bf16[64,128,256]{2,1,0:T(8,128)(2,1)S(1)} %get-tuple-element.9.s_in, f32[128,128]{1,0:T(8,128)S(1)} %get-tuple-element.10.total_v, f32[8,128]{1,0:T(8,128)S(1)} %get-tuple-element.11.tail_v, f32[1,64]{1,0:T(1,128)S(1)} %bitcast.2, ...), custom_call_target="tpu_custom_call" | custom-call | flops 1000000 | bytes 8388608 | tf_op jit(solution)/shard_map/pallas_call | solution.py:716
Async XLA Ops:
  0.6 59.9 %copy-start = (f32[64,64]{1,0:T(8,128)S(1)}, f32[64,64]{1,0:T(8,128)}, u32[]{:S(2)}) copy-start(f32[64,64]{1,0:T(8,128)} %wgt_v.1) | copy-start | bytes 49156
  0.6 59.9 %copy-start.1 = (f32[64]{0:T(128)S(1)}, f32[64]{0:T(128)}, u32[]{:S(2)}) copy-start(f32[64]{0:T(128)} %coef_h.1) | copy-start | bytes 772

commit v6 on v5

--- a/solution.py
+++ b/solution.py
@@ -12,9 +12,9 @@
 MESH = pl.DeviceIdType.MESH
 F32 = jnp.float32
 BF16 = jnp.bfloat16
-CH = 8
+CH = 4
 SUB = 8
-LAG = 1
+LAG = 2
 COV_BLOCKS = ((0, 32), (32, 16), (48, 16))
 JAC_BLOCK = 32
 TAIL = 32

time: 63.3 us -> 60.7 us (0.959)
  Pallas kernels: 62.5 us -> 60 us
    pallas_call x1, Pallas kernels: 59.8 us -> 57.3 us  [local(): pl.pallas_call(functools.partial(kernel, nx, ny), out_shape=(pltpu.VMEM((...]
where the time goes in v6:
time: 60.7 us; the launch traced here: 60.6 us
  Pallas kernels  60 us (99%)
  between operations  0.67 us (1%)
    pallas_call x1, Pallas kernels, local(): pl.pallas_call(functools.partial(kernel, nx, ny), out_shape=(pltpu.VMEM((...  57.3 us
    pallas_call x1, Pallas kernels, local(): pl.pallas_call(finish, out_shape=(jax.ShapeDtypeStruct((channels, rows, c...  2.66 us

profile of v6, /device:TPU:1, one launch (start us, length us, event | category | flops | bytes accessed | tf_op | source)
XLA Modules:
  0.0 60.6 jit_solution(7146034684772391071)
XLA Ops:
  0.6 0.0 copy-start
  0.6 0.0 copy-start.1
  0.7 57.3 %shard_map.85 = (bf16[64,128,256]{2,1,0:T(8,128)(2,1)S(1)}, f32[128,128]{1,0:T(8,128)S(1)}, f32[8,128]{1,0:T(8,128)S(1)}) custom-call(bf16[64,128,256]{2,1,0:T(8,128)(2,1)} %inst_h.1, bf16[64,128,256]{2,1,0:T(8,128)(2,1)} %reg_h.1, f32[128,256]{1,0:T(8,128)} %outcome_h.1, s32[128,256]{1,0:T(8,128)} %land_h.1, f32[64]{0:T(128)} %coef_h.1), custom_call_target="tpu_custom_call" | custom-call | flops 5000000000 | bytes 13631488 | tf_op jit(solution)/shard_map/pallas_call | solution.py:658
  58.0 0.0 copy-done
  58.0 0.0 copy-done.1
  58.0 2.7 %shard_map.86 = (bf16[64,128,256]{2,1,0:T(8,128)(2,1)}, f32[64,64]{1,0:T(8,128)}, f32[1,64]{1,0:T(1,128)}) custom-call(bf16[64,128,256]{2,1,0:T(8,128)(2,1)S(1)} %get-tuple-element.9.s_in, f32[128,128]{1,0:T(8,128)S(1)} %get-tuple-element.10.total_v, f32[8,128]{1,0:T(8,128)S(1)} %get-tuple-element.11.tail_v, f32[1,64]{1,0:T(1,128)S(1)} %bitcast.2, ...), custom_call_target="tpu_custom_call" | custom-call | flops 1000000 | bytes 8388608 | tf_op jit(solution)/shard_map/pallas_call | solution.py:716
Async XLA Ops:
  0.6 57.3 %copy-start = (f32[64,64]{1,0:T(8,128)S(1)}, f32[64,64]{1,0:T(8,128)}, u32[]{:S(2)}) copy-start(f32[64,64]{1,0:T(8,128)} %wgt_v.1) | copy-start | bytes 49156
  0.6 57.3 %copy-start.1 = (f32[64]{0:T(128)S(1)}, f32[64]{0:T(128)}, u32[]{:S(2)}) copy-start(f32[64]{0:T(128)} %coef_h.1) | copy-start | bytes 772
